TPU v7x, 256 devices: a whole 4x4x8 slice. The times are simulated.
256 devices in a mesh: lon: 16 (over z, core), lat: 16 (over x, y).
Axes of the slice: x: 4, y: 4, z: 8, core: 2. Of those that a mesh axis runs over, the one named last changes fastest.
Arguments:
- state: float32 [3, 16, 512, 4096], P(None, None, 'lat', 'lon'), may hold values from -6 to 6
- kmt: int32 [512, 4096], P('lat', 'lon'), may hold values from 0 to 16, as said below
- first_guess: float32 [512, 4096], P('lat', 'lon'), may hold values from -6 to 6
Outputs:
- next_state: float32 [3, 16, 512, 4096], P(None, None, 'lat', 'lon')
- pressure: float32 [512, 4096], P('lat', 'lon')
Inputs may be any that keep to these rules, and one draw needn't show every extreme that they name: `kmt`: 0 marks a land column.
All inputs are finite; a program needn't handle non-finite values.
Results may differ from a plain program's by a relative error of at most 0.0001.
Values sent between devices are 32-bit elements; how exact they have to be, the bound alone decides.
No kernel may reach another device: no remote copies, remote signals or barrier semaphores. Data moves between devices by JAX's collectives and lax.ppermute only.
A program may use at most 64 MiB of HBM per device.

v0:
```python
import jax
import jax.numpy as jnp
from jax import lax
from jax.experimental import pallas as pl
from jax.experimental.pallas import tpu as pltpu
from jax.sharding import PartitionSpec as P

ITERS = 4
F32 = jnp.float32

viscosity = 0.12
diffusivity = 0.1
advection_scale = 0.5
vertical_mix = 0.2
coriolis_scale = 0.6
time_step = 0.5
storage = 0.5
gravity = 1.5
edge_weight = 2.0 / 3.0
corner_weight = 1.0 / 6.0

TILE = 8
LANES = 128
LEVELS = LANES // TILE
HALO = 6

U_ROWS = 0
V_ROWS = U_ROWS + LEVELS // 4
T_ROWS = V_ROWS + LEVELS // 4
KMT, GUESS, SUM_U, SUM_V, STRIPS = range(T_ROWS + LEVELS // 8, T_ROWS + LEVELS // 8 + 5)
SLOTS = STRIPS + 3

LOWEST = storage / (storage + 4 * edge_weight + 4 * corner_weight)
HIGHEST = 2.0 - LOWEST
VMEM_LIMIT = 16 * 1024 * 1024
VMEM_FIRST = 64520000


def params(limit=VMEM_LIMIT):
    return pltpu.CompilerParams(vmem_limit_bytes=limit)


def cost(size):
    return pl.CostEstimate(flops=60 * size, bytes_accessed=8 * size, transcendentals=0)


def turn(x, shift, axis):
    return pltpu.roll(x, shift % x.shape[axis], axis)


def east_of(x):
    return turn(x, -1, 1)


def west_of(x):
    return turn(x, 1, 1)


def north_of(x):
    return turn(x, -1, 0)


def south_of(x):
    return turn(x, 1, 0)


def lane_of(shape):
    return lax.broadcasted_iota(jnp.int32, shape, len(shape) - 1)


def is_even(axis):
    return lax.rem(lax.axis_index(axis), 2) == 0


def swap(first, a, b):
    return jnp.where(first, a, b), jnp.where(first, b, a)


def stacked(south, own, north):
    return jnp.concatenate([south, own, north], axis=0)


def place(group, k, west, east, acc):
    to_west, to_east = acc
    to_west = jnp.where(group == k, pltpu.roll(west, 2 + TILE * k, 1), to_west)
    to_east = jnp.where(
        group == k, pltpu.roll(east, lax.rem(HALO + TILE * k, LANES), 1), to_east
    )
    return to_west, to_east


def pack_own(state, kmt, guess, strips):
    levels, rows_here, breadth = state.shape[1:]
    group = lane_of((rows_here, LANES)) // TILE
    ends = slice(0, LANES), slice(breadth - LANES, breadth)
    blank = (jnp.zeros((rows_here, LANES), F32),) * 2
    for field in range(3):

        def body(k, acc, field=field):
            west, east = [state[field, k, :, cols] for cols in ends]
            return place(group, k, west, east, acc)

        acc = lax.fori_loop(0, levels, body, blank, unroll=4)
        strips[0, field], strips[1, field] = acc
    acc = blank
    for number, own in enumerate((kmt[...].astype(F32), guess[...])):
        west, east = [own[:, cols] for cols in ends]
        acc = place(group, jnp.int32(number), west, east, acc)
    strips[0, 3], strips[1, 3] = acc


def pack_cols(strips, rows_odd, rows_even, msg_odd, msg_even):
    tall = strips.shape[2] + 2 * TILE
    lat_even = is_even("lat")
    lon_even = is_even("lon")

    def put(number, field, south, north):
        base = number * tall
        to_west, to_east = (
            stacked(
                south[:, i * LANES : (i + 1) * LANES],
                strips[i, field],
                north[:, i * LANES : (i + 1) * LANES],
            )
            for i in range(2)
        )
        a, b = swap(lon_even, to_east, to_west)
        msg_even[base : base + tall] = a
        msg_odd[base : base + tall] = b

    halos = []
    for slot in range(STRIPS, SLOTS):
        north, south = swap(lat_even, rows_even[slot], rows_odd[slot])
        halos.append((south, north))
    put(0, 0, *halos[0])
    put(1, 1, *halos[1])
    put(2, 3, *halos[2])
    put(3, 2, turn(halos[0][0], -1, 0), turn(halos[0][1], 1, 0))


def rotation_at(row, rows_here):
    total_rows = rows_here * lax.axis_size("lat")
    row = (row + lax.axis_index("lat") * rows_here).astype(F32)
    angle = jnp.pi / 180.0 * (-80.0 + 160.0 * (row + 0.5) / total_rows)
    return coriolis_scale * jnp.sin(angle)


def around(x):
    return east_of(x), west_of(x), north_of(x), south_of(x)


def count_wet(sides, level):
    total = None
    for side in sides:
        term = jnp.where(side > level, 1.0, 0.0)
        total = term if total is None else total + term
    return total


def spread(x, sides, count, coefficient, zonal, merid):
    east, west, north, south = sides
    laplace = east + west + north + south - count * x
    return (
        (time_step * coefficient) * laplace
        - zonal * (east - west)
        - merid * (north - south)
    )


carry = 0.5 * time_step * advection_scale


def advance_flow(u, v, wet, count, half_turn):
    zonal, merid = (carry * u, carry * v)
    new_u = u + (spread(u, around(u), count, viscosity, zonal, merid) + half_turn * v)
    new_v = v + (spread(v, around(v), count, viscosity, zonal, merid) - half_turn * u)
    return jnp.where(wet, new_u, 0.0), jnp.where(wet, new_v, 0.0)


def pack_rows(state, kmt, guess, msg_odd, msg_even, ends, wet_ends, guess_ends, sems):
    levels, rows_here, breadth = state.shape[1:]
    even = is_even("lat")
    copies = []
    for number, rows in enumerate((slice(0, TILE), slice(rows_here - TILE, rows_here))):
        held = slice(number * TILE, (number + 1) * TILE)
        for source, target in (
            (state.at[:, :, rows, :], ends.at[:, :, held, :]),
            (kmt.at[rows, :], wet_ends.at[held, :]),
            (guess.at[rows, :], guess_ends.at[held, :]),
        ):
            copies.append(pltpu.make_async_copy(source, target, sems.at[len(copies)]))
            copies[-1].start()
    row = lax.broadcasted_iota(jnp.int32, (2 * TILE, LANES), 0)
    rotation = rotation_at(jnp.where(row < TILE, row, row + rows_here - 2 * TILE), rows_here)
    half_turn = time_step * rotation[:, :1]
    group = lane_of((2 * TILE, LANES)) // TILE
    row = lax.broadcasted_iota(jnp.int32, (2 * TILE, breadth), 0)
    borrowed = (row == TILE - 1) | (row == TILE)
    for item in copies:
        item.wait()

    depth = wet_ends[...].astype(F32)
    beside = around(depth)
    cut = slice(0, LANES), slice(breadth - LANES, breadth)

    def body(k, carried):
        sum_u, sum_v, strips_u, strips_v = carried
        level = k.astype(F32)
        wet = depth > level
        raw_u, raw_v, raw_t = [ends[field, k] for field in range(3)]
        u = jnp.where(wet, raw_u, 0.0)
        v = jnp.where(wet, raw_v, 0.0)
        new_u, new_v = advance_flow(u, v, wet, count_wet(beside, level), half_turn)
        moved = jnp.concatenate([turn(raw_t[:TILE], -1, 0), turn(raw_t[TILE:], 1, 0)], axis=0)
        lent = jnp.where(borrowed, moved, raw_u)
        strips_u = place(group, k, lent[:, cut[0]], lent[:, cut[1]], strips_u)
        strips_v = place(group, k, raw_v[:, cut[0]], raw_v[:, cut[1]], strips_v)
        return sum_u + new_u, sum_v + new_v, strips_u, strips_v

    empty = jnp.zeros((2 * TILE, breadth), F32)
    blank = (jnp.zeros((2 * TILE, LANES), F32),) * 2
    sum_u, sum_v, strips_u, strips_v = lax.fori_loop(
        0, levels, body, (empty, empty, blank, blank), unroll=2
    )
    starts = guess_ends[...]
    others = blank
    for number, value in enumerate((depth, starts)):
        others = place(group, jnp.int32(number), value[:, cut[0]], value[:, cut[1]], others)

    def put(slot, low, high):
        a, b = swap(even, high, low)
        msg_even[slot] = a
        msg_odd[slot] = b

    whole = [depth, starts, sum_u, sum_v]
    whole += [jnp.concatenate(pair, axis=1) for pair in (strips_u, strips_v, others)]
    for slot, value in enumerate(whole, KMT):
        put(slot, value[:TILE], value[TILE:])
    row = lax.broadcasted_iota(jnp.int32, (TILE, breadth), 0)
    for field, first, width in ((0, U_ROWS, 2), (1, V_ROWS, 2), (2, T_ROWS, 1)):
        each = TILE // width
        for tile in range(levels // each):
            low = high = jnp.zeros((TILE, breadth), F32)
            for q in range(each):
                value = ends[field, tile * each + q]
                here = row // width == q
                low = jnp.where(here, turn(value[:TILE], width * q, 0), low)
                high = jnp.where(here, turn(value[TILE:], width * (q + 1), 0), high)
            put(first + tile, low, high)


def halo_rows(rows_even, rows_odd, first, width, k):
    each = TILE // width
    tile = first + k // each
    north, south = swap(is_even("lat"), rows_even[tile], rows_odd[tile])
    at = lax.rem(k, each) * width
    south = pltpu.roll(south, lax.rem(2 * TILE - width - at, TILE), 0)
    north = pltpu.roll(north, lax.rem(TILE - at, TILE), 0)
    return south, north


def advance_inner(state, kmt, rows_odd, rows_even, flow, tracer, flow_u, flow_v, turning):
    levels, rows_here, breadth = state.shape[1:]
    tall = rows_here + 2 * TILE
    lat_even = is_even("lat")

    def halos(slot):
        north, south = swap(lat_even, rows_even[slot], rows_odd[slot])
        return south, north

    south, north = halos(KMT)
    depth = stacked(south, kmt[...].astype(F32), north)
    beside = around(depth)
    row = lax.broadcasted_iota(jnp.int32, (tall, LANES), 0)
    rotation = rotation_at(row - TILE, rows_here)
    turning[...] = rotation
    half_turn = time_step * rotation[:, :1]
    own = slice(TILE, TILE + rows_here)
    flow_u[...] = jnp.zeros_like(flow_u)
    flow_v[...] = jnp.zeros_like(flow_v)

    def body(k, _):
        level = k.astype(F32)
        wet = depth > level
        count = count_wet(beside, level)
        u_south, u_north = halo_rows(rows_even, rows_odd, U_ROWS, 2, k)
        v_south, v_north = halo_rows(rows_even, rows_odd, V_ROWS, 2, k)
        t_south, t_north = halo_rows(rows_even, rows_odd, T_ROWS, 1, k)
        u = jnp.where(wet, stacked(u_south, state[0, k], u_north), 0.0)
        v = jnp.where(wet, stacked(v_south, state[1, k], v_north), 0.0)
        new_u, new_v = advance_flow(u, v, wet, count, half_turn)
        flow_u[...] += new_u
        flow_v[...] += new_v
        flow[0, k] = new_u[own]
        flow[1, k] = new_v[own]
        here = state[2, k]
        stack_t = jnp.where(wet, stacked(t_south, here, t_north), 0.0)
        middle = stack_t[own]
        sides = (east_of(middle), west_of(middle), north_of(stack_t)[own], south_of(stack_t)[own])
        change = spread(
            middle, sides, count[own], diffusivity, carry * u[own], carry * v[own]
        )
        above = state[2, jnp.maximum(k - 1, 0)]
        below = state[2, jnp.minimum(k + 1, levels - 1)]
        vertical = (above - here) + jnp.where(depth[own] > level + 1.0, below - here, 0.0)
        tracer[k] = jnp.where(
            wet[own], here + (change + (time_step * vertical_mix) * vertical), 0.0
        )
        return 0

    lax.fori_loop(0, levels, body, 0)
    row = lax.broadcasted_iota(jnp.int32, (tall, breadth), 0)
    outer = (row < TILE - 1) | (row > TILE + rows_here)
    inner = jnp.zeros((rows_here, breadth), F32)
    for slot, flow_sum in ((SUM_U, flow_u), (SUM_V, flow_v)):
        south, north = halos(slot)
        flow_sum[...] = jnp.where(outer, stacked(south, inner, north), flow_sum[...])


def fill_ends(x, west, east):
    lane = lane_of((x.shape[0], LANES))
    tiles = [x[:, i : i + LANES] for i in range(0, x.shape[1], LANES)]
    if west is not None:
        tiles[0] = jnp.where(lane == 0, west, tiles[0])
    if east is not None:
        tiles[-1] = jnp.where(lane == LANES - 1, east, tiles[-1])
    return jnp.concatenate(tiles, axis=1)


def roll_to(x, source, target, k):
    return turn(x, target - source - TILE * k, 1)


def over_groups(x):
    for step in (TILE, 2 * TILE, 4 * TILE, 8 * TILE):
        x = x + pltpu.roll(x, step, 1)
    return x


def krylov(
    sent_even, sent_odd, got_odd, got_even, flow_u, flow_v, kmt, guess,
    rows_even, rows_odd, turning, edges, basis, moments,
):
    levels = LEVELS
    rows_here, breadth = kmt.shape
    tall = rows_here + 2 * TILE
    lat_even = is_even("lat")
    lon_even = is_even("lon")
    lane = lane_of((tall, LANES))
    place = lax.rem(lane, TILE)
    group = lane // TILE
    level = group.astype(F32)
    own = slice(TILE, TILE + rows_here)
    half_turn = time_step * turning[...]

    def strips(slot):
        rows = slice(slot * tall, (slot + 1) * tall)
        to_east, to_west = swap(lon_even, sent_even[rows], sent_odd[rows])
        from_east, from_west = swap(lon_even, got_even[rows], got_odd[rows])
        west = jnp.where(place < HALO, from_west, turn(to_west, 4, 1))
        east = jnp.where(place >= TILE - HALO, from_east, turn(to_east, -4, 1))
        return west, east

    u_sides, v_sides, other = [strips(slot) for slot in range(3)]
    t_sides = strips(3)
    sums = []
    for side in range(2):
        depth = over_groups(jnp.where(group == 0, other[side], 0.0))
        start = over_groups(jnp.where(group == 1, other[side], 0.0))
        wet = depth > level
        count = count_wet(around(depth), level)
        u = jnp.where(wet, u_sides[side], 0.0)
        v = jnp.where(wet, v_sides[side], 0.0)
        new_u, new_v = advance_flow(u, v, wet, count, half_turn)
        here = jnp.where(wet, t_sides[side], 0.0)
        change = spread(here, around(here), count, diffusivity, carry * u, carry * v)
        above = jnp.where(group > 0, turn(here, TILE, 1) - here, 0.0)
        below = jnp.where(depth > level + 1.0, turn(here, -TILE, 1) - here, 0.0)
        new_t = jnp.where(
            wet, here + (change + (time_step * vertical_mix) * (above + below)), 0.0
        )
        edges[side, 0] = new_u[own]
        edges[side, 1] = new_v[own]
        edges[side, 2] = new_t[own]
        sums.append((over_groups(new_u), over_groups(new_v), depth, start))

    def assemble(field, number, seam):
        west = turn(sums[0][number], 2, 1)
        east = turn(sums[1][number], -2, 1)
        halo = jnp.where(lane < LANES // 2, east, west)
        tiles = [field[:, i : i + LANES] for i in range(0, breadth, LANES)]
        if seam:
            tiles[0] = jnp.where(lane == 0, west, tiles[0])
            tiles[-1] = jnp.where(lane == LANES - 1, east, tiles[-1])
        return jnp.concatenate(tiles + [halo], axis=1)

    def tall_field(slot, value):
        north, south = swap(lat_even, rows_even[slot], rows_odd[slot])
        return stacked(south, value, north)

    wide_u = assemble(flow_u[...], 0, True)
    wide_v = assemble(flow_v[...], 1, True)
    wet_levels = assemble(tall_field(KMT, kmt[...].astype(F32)), 2, False)
    first = assemble(tall_field(GUESS, guess[...]), 3, False)

    divergence = 0.5 * (east_of(wide_u) - west_of(wide_u)) + 0.5 * (
        north_of(wide_v) - south_of(wide_v)
    )
    depth = wet_levels * (1.0 / levels)
    ocean = wet_levels > 0.0
    to_east = edge_weight * jnp.minimum(depth, east_of(depth))
    to_north = edge_weight * jnp.minimum(depth, north_of(depth))
    depth_north = north_of(depth)
    to_ne = corner_weight * jnp.minimum(depth, east_of(depth_north))
    to_nw = corner_weight * jnp.minimum(depth, west_of(depth_north))
    to_west = west_of(to_east)
    to_south = south_of(to_north)
    to_sw = south_of(west_of(to_ne))
    to_se = south_of(east_of(to_nw))
    diagonal = storage + (
        (to_east + to_west) + (to_north + to_south) + ((to_ne + to_nw) + (to_se + to_sw))
    )

    def neighbours(x):
        up, down = (north_of(x), south_of(x))
        eastern = to_east * x + to_ne_w * up + to_se_w * down
        western = to_west * x + to_nw_e * up + to_sw_e * down
        return to_north * up + to_south * down + (east_of(eastern) + west_of(western))

    to_ne_w = west_of(to_ne)
    to_se_w = west_of(to_se)
    to_nw_e = east_of(to_nw)
    to_sw_e = east_of(to_sw)
    to_east, to_west = (west_of(to_east), east_of(to_west))

    start = jnp.where(ocean, first, 0.0)
    rhs = jnp.where(ocean, storage * (start - time_step * divergence), 0.0)
    residual = rhs - (diagonal * start - neighbours(start))
    inverse = 1.0 / diagonal
    vectors = [residual * inverse]
    basis[0] = start
    basis[1] = vectors[0]
    for k in range(1, ITERS):
        vectors.append(neighbours(vectors[-1]) * inverse)
        basis[k + 1] = vectors[k]
    last = neighbours(vectors[-1])

    def inner(x):
        return x[own, :breadth]

    weighted = [inner(diagonal * x) for x in vectors] + [inner(last)]
    held = [inner(x) for x in vectors]
    slot = lane_of((1, LANES))
    total = jnp.zeros((1, LANES), F32)
    for m in range(2 * ITERS):
        product = held[m // 2] * weighted[(m + 1) // 2]
        total = jnp.where(slot == m, jnp.sum(product), total)
    moments[...] = total


def finish(shares, basis, edges, kmt, flow, tracer, out, pressure, done, sems):
    levels, rows_here, breadth = tracer.shape
    own = slice(TILE, TILE + rows_here)
    chunks = sems.shape[1]
    size = levels // chunks

    def send(first, last, c):
        part = pl.ds(c * size, size)
        fields = slice(first, last)
        return pltpu.make_async_copy(
            done.at[fields, part], out.at[fields, part], sems.at[first // 2, c]
        )

    def ended(value, field, k):
        return fill_ends(
            value,
            roll_to(edges[0, field], HALO, 0, k),
            roll_to(edges[1, field], 1, LANES - 1, k),
        )

    for c in range(chunks):
        for k in range(c * size, (c + 1) * size):
            done[2, k] = ended(tracer[k], 2, k)
        send(2, 3, c).start()
    sums = jnp.sum(shares[...], axis=0, keepdims=True)
    res = [sums[:, m : m + 1] for m in range(2 * ITERS)]
    dirn = list(res)
    one, zero = (jnp.ones((1, 1), F32), jnp.zeros((1, 1), F32))
    res_in = [one] + [zero] * (ITERS - 1)
    dir_in = list(res_in)
    height_in = [zero] * ITERS
    for k in range(ITERS):
        step = res[k] / (dirn[k] - dirn[k + 1])
        step = jnp.clip(step, 1.0 / HIGHEST, 1.0 / LOWEST)
        height_in = [h + step * d for h, d in zip(height_in, dir_in)]
        if k + 1 < ITERS:
            new = [res[m] - step * (dirn[m] - dirn[m + 1]) for m in range(len(dirn) - 1)]
            ratio = jnp.clip(step * new[k + 1] / res[k], 0.0, HIGHEST / LOWEST)
            dirn = [n + ratio * d for n, d in zip(new, dirn)]
            res = new
            moved = [zero] + dir_in[:-1]
            res_in = [r - step * (d - m) for r, d, m in zip(res_in, dir_in, moved)]
            dir_in = [r + ratio * d for r, d in zip(res_in, dir_in)]
    height = basis[0]
    for k in range(ITERS):
        height = height + height_in[k] * basis[k + 1]
    pressure[...] = gravity * height[own, :breadth]
    pull = 0.5 * time_step * gravity
    slope_east = pull * (east_of(height) - west_of(height))[own, :breadth]
    slope_north = pull * (north_of(height) - south_of(height))[own, :breadth]
    wet_levels = kmt[...]
    for c in range(chunks):
        for k in range(c * size, (c + 1) * size):
            wet = wet_levels > k
            for field, slope in ((0, slope_east), (1, slope_north)):
                done[field, k] = jnp.where(wet, ended(flow[field, k], field, k) - slope, 0.0)
        send(0, 2, c).start()
    for c in range(chunks):
        send(2, 3, c).wait()
        send(0, 2, c).wait()


def pairs(axis):
    peers = lax.axis_size(axis)
    even = [(i, i ^ 1) for i in range(peers)]
    odd = [(i, ((i + 1) ^ 1) - 1) for i in range(1, peers - 1)]
    if axis == "lon":
        odd += [(0, peers - 1), (peers - 1, 0)]
    return even, odd


def exchange(axis, to_even, to_odd):
    even, odd = pairs(axis)
    from_odd = lax.ppermute(to_odd, axis, odd)
    return lax.ppermute(to_even, axis, even), from_odd


def on_device(state, kmt, first_guess):
    _, levels, rows_here, breadth = state.shape
    tall = rows_here + 2 * TILE
    wide = breadth + LANES
    shape = lambda *dims: jax.ShapeDtypeStruct(dims, F32)

    devices = lax.axis_size("lon") * lax.axis_size("lat")
    hbm = pl.BlockSpec(memory_space=pltpu.HBM)
    vmem = pl.BlockSpec(memory_space=pltpu.VMEM)
    to_odd, to_even = pl.pallas_call(
        pack_rows,
        in_specs=[hbm] * 3,
        out_specs=[vmem] * 2,
        out_shape=[shape(SLOTS, TILE, breadth)] * 2,
        scratch_shapes=[
            pltpu.VMEM((3, levels, 2 * TILE, breadth), F32),
            pltpu.VMEM((2 * TILE, breadth), jnp.int32),
            pltpu.VMEM((2 * TILE, breadth), F32),
            pltpu.SemaphoreType.DMA((6,)),
        ],
        compiler_params=params(VMEM_FIRST),
    )(state, kmt, first_guess)
    rows_even, rows_odd = exchange("lat", to_even, to_odd)

    strips = pl.pallas_call(
        pack_own,
        out_shape=shape(2, 4, rows_here, LANES),
        compiler_params=params(),
        cost_estimate=cost(state.size),
    )(state, kmt, first_guess)
    length = 4 * tall
    sent_odd, sent_even = pl.pallas_call(
        pack_cols,
        out_shape=[shape(length, LANES)] * 2,
        compiler_params=params(),
    )(strips, rows_odd, rows_even)
    got_even, got_odd = exchange("lon", sent_even, sent_odd)

    flow, tracer, flow_u, flow_v, turning = pl.pallas_call(
        advance_inner,
        out_shape=[
            shape(2, levels, rows_here, breadth),
            shape(levels, rows_here, breadth),
            shape(tall, breadth),
            shape(tall, breadth),
            shape(tall, LANES),
        ],
        compiler_params=params(),
        cost_estimate=cost(state.size),
    )(state, kmt, rows_odd, rows_even)

    edges, basis, moments = pl.pallas_call(
        krylov,
        out_shape=[
            shape(2, 3, rows_here, LANES),
            shape(ITERS + 1, tall, wide),
            shape(1, LANES),
        ],
        compiler_params=params(),
    )(
        sent_even, sent_odd, got_odd, got_even, flow_u, flow_v, kmt, first_guess,
        rows_even, rows_odd, turning,
    )

    shares = jnp.broadcast_to(moments[None], (devices, 1, LANES))
    shares = lax.all_to_all(shares, ("lon", "lat"), 0, 0)
    return pl.pallas_call(
        finish,
        in_specs=[vmem] * 6,
        out_specs=[hbm, vmem],
        out_shape=[shape(3, levels, rows_here, breadth), shape(rows_here, breadth)],
        scratch_shapes=[
            pltpu.VMEM((3, levels, rows_here, breadth), F32),
            pltpu.SemaphoreType.DMA((2, 4)),
        ],
        compiler_params=params(),
    )(shares.reshape(devices, LANES), basis, edges, kmt, flow, tracer)


def solution(mesh):
    placed = (P(None, None, "lat", "lon"), P("lat", "lon"), P("lat", "lon"))
    return jax.shard_map(
        on_device,
        mesh=mesh,
        in_specs=placed,
        out_specs=(P(None, None, "lat", "lon"), P("lat", "lon")),
        check_vma=False,
    )
```

profile of v0, /device:TPU:1, one launch (start us, length us, event | category | flops | bytes accessed | tf_op | source)
XLA Modules:
  0.0 52.3 jit_solution(11906219040990168838)
XLA Ops:
  0.6 0.0 copy-start.1
  0.6 0.0 copy-start.2
  0.6 0.0 copy-start
  0.7 3.2 %shard_map.51 = (f32[17,8,256]{2,1,0:T(8,128)}, f32[17,8,256]{2,1,0:T(8,128)}) custom-call(f32[3,16,32,256]{3,2,1,0:T(8,128)} %state.5, s32[32,256]{1,0:T(8,128)} %kmt.9, f32[32,256]{1,0:T(8,128)} %guess.5), custom_call_target="tpu_custom_call" | custom-call | tf_op jit(solution)/shard_map/pallas_call | solution.py:547
  3.8 0.7 %collective-permute-start = (f32[17,8,256]{2,1,0:T(8,128)}, f32[17,8,256]{2,1,0:T(8,128)S(1)}, u32[]{:S(2)}, u32[]{:S(2)}) collective-permute-start(f32[17,8,256]{2,1,0:T(8,128)} %get-tuple-element.14), channel_id=1, source_target_pairs={{1,2},{2,1},{3,4},{4,3},{5,6},{6,5},{7,8},{8,7},{9,10},{10,9},{11,... | collective-permute-start | bytes 417800 | tf_op jit(solution)/shard_map/ppermute | solution.py:534
  4.5 4.7 %collective-permute-start.1 = (f32[17,8,256]{2,1,0:T(8,128)}, f32[17,8,256]{2,1,0:T(8,128)S(1)}, u32[]{:S(2)}, u32[]{:S(2)}) collective-permute-start(f32[17,8,256]{2,1,0:T(8,128)} %get-tuple-element.15), channel_id=1, source_target_pairs={{0,1},{1,0},{2,3},{3,2},{4,5},{5,4},{6,7},{7,6},{8,9},{9,8},{10,11... | collective-permute-start | bytes 417800 | tf_op jit(solution)/shard_map/ppermute | solution.py:535
  9.3 0.0 copy-done.1
  9.3 0.0 copy-done.2
  9.3 0.0 copy-done
  9.3 1.3 %shard_map.50.strips = f32[2,4,32,128]{3,2,1,0:T(8,128)S(1)} custom-call(f32[3,16,32,256]{3,2,1,0:T(8,128)S(1)} %copy-done, s32[32,256]{1,0:T(8,128)S(1)} %copy-done.1, f32[32,256]{1,0:T(8,128)S(1)} %copy-done.2), custom_call_target="tpu_custom_call" | custom-call | flops 23592960 | bytes 3145728 | tf_op jit(solution)/shard_map/pallas_call | solution.py:562
  10.6 0.0 collective-permute-done.rows_odd
  10.6 2.0 %collective-permute-done.1.rows_even = f32[17,8,256]{2,1,0:T(8,128)S(1)} collective-permute-done((f32[17,8,256]{2,1,0:T(8,128)}, f32[17,8,256]{2,1,0:T(8,128)S(1)}, u32[]{:S(2)}, u32[]{:S(2)}) %collective-permute-start.1) | collective-permute-done | bytes 139296 | tf_op jit(solution)/shard_map/ppermute | solution.py:535
  12.6 1.6 %collective-permute-start.3 = (f32[192,128]{1,0:T(8,128)S(1)}, f32[192,128]{1,0:T(8,128)S(1)}, u32[]{:S(2)}, u32[]{:S(2)}) collective-permute-start(f32[192,128]{1,0:T(8,128)S(1)} %get-tuple-element.16.sent_even), channel_id=1, source_target_pairs={{0,16},{16,0},{32,48},{48,32},{64,80},{80,64},{96,112},{112,96},{1... | collective-permute-start | bytes 294920 | tf_op jit(solution)/shard_map/ppermute | solution.py:535
  14.2 1.6 %collective-permute-start.2 = (f32[192,128]{1,0:T(8,128)S(1)}, f32[192,128]{1,0:T(8,128)S(1)}, u32[]{:S(2)}, u32[]{:S(2)}) collective-permute-start(f32[192,128]{1,0:T(8,128)S(1)} %get-tuple-element.17.sent_odd), channel_id=1, source_target_pairs={{16,32},{32,16},{48,64},{64,48},{80,96},{96,80},{112,128},{128,112... | collective-permute-start | bytes 294920 | tf_op jit(solution)/shard_map/ppermute | solution.py:534
  15.8 3.1 %shard_map.53 = (f32[2,16,32,256]{3,2,1,0:T(8,128)S(1)}, f32[16,32,256]{2,1,0:T(8,128)S(1)}, f32[48,256]{1,0:T(8,128)S(1)}, f32[48,256]{1,0:T(8,128)S(1)}, f32[48,128]{1,0:T(8,128)S(1)}) custom-call(f32[3,16,32,256]{3,2,1,0:T(8,128)S(1)} %copy-done, s32[32,256]{1,0:T(8,128)S(1)} %copy-done.1, f32[17,8,256]{2,1,0:T(8,128)S(1)} %collective-permute-done.rows_odd, ...), custom_call_target="tpu_custom_call" | custom-call | flops 23592960 | bytes 3145728 | tf_op jit(solution)/shard_map/pallas_call | solution.py:576
  19.0 0.0 collective-permute-done.3.got_even
  19.0 0.0 collective-permute-done.2.got_odd
  19.0 1.7 %shard_map.54 = (f32[2,3,32,128]{3,2,1,0:T(8,128)S(1)}, f32[5,48,384]{2,1,0:T(8,128)S(1)}, f32[1,128]{1,0:T(1,128)S(1)}) custom-call(f32[192,128]{1,0:T(8,128)S(1)} %get-tuple-element.16.sent_even, f32[192,128]{1,0:T(8,128)S(1)} %get-tuple-element.17.sent_odd, f32[192,128]{1,0:T(8,128)S(1)} %collective-permute-done.2.got_odd, ...), custom_call_target="tpu_custom_call" | custom-call | tf_op jit(solution)/shard_map/pallas_call | solution.py:589
  20.7 0.1 broadcast_in_dim.9
  20.8 28.3 %all_to_all.5 = f32[256,1,128]{2,1,0:T(1,128)S(1)} all-to-all(f32[256,1,128]{2,1,0:T(1,128)S(1)} %broadcast_in_dim.9), channel_id=1, replica_groups=mesh['lon'=16,'lat'=16] {'lon','lat'}, dimensions={0} | all-to-all | bytes 262144 | tf_op jit(solution)/shard_map/all_to_all | solution.py:603
  49.1 3.2 %shard_map.55 = (f32[3,16,32,256]{3,2,1,0:T(8,128)}, f32[32,256]{1,0:T(8,128)}) custom-call(f32[256,128]{1,0:T(8,128)S(1)} %bitcast.2, f32[5,48,384]{2,1,0:T(8,128)S(1)} %get-tuple-element.22.basis, f32[2,3,32,128]{3,2,1,0:T(8,128)S(1)} %get-tuple-element.23.edges, s32[32,256]{1,0:T(8,128)S(1)} %copy-done.1, f32[2,16,32,256]{3,2,1,0:T(8,128)S(1)} %get-tuple-element.24.flow, ...), custom_call_target="tpu_custom_call" | custom-call | tf_op jit(solution)/shard_map/pallas_call | solution.py:604
  (1 shorter events, 0.0 us)
Async XLA Ops:
  0.6 8.6 %copy-start.1 = (s32[32,256]{1,0:T(8,128)S(1)}, s32[32,256]{1,0:T(8,128)}, u32[]{:S(2)}) copy-start(s32[32,256]{1,0:T(8,128)} %kmt.9) | copy-start | bytes 98308
  0.6 8.6 %copy-start.2 = (f32[32,256]{1,0:T(8,128)S(1)}, f32[32,256]{1,0:T(8,128)}, u32[]{:S(2)}) copy-start(f32[32,256]{1,0:T(8,128)} %guess.5) | copy-start | bytes 98308
  0.6 8.6 %copy-start = (f32[3,16,32,256]{3,2,1,0:T(8,128)S(1)}, f32[3,16,32,256]{3,2,1,0:T(8,128)}, u32[]{:S(2)}) copy-start(f32[3,16,32,256]{3,2,1,0:T(8,128)} %state.5) | copy-start | bytes 4718596
  3.8 6.8 %collective-permute-start = (f32[17,8,256]{2,1,0:T(8,128)}, f32[17,8,256]{2,1,0:T(8,128)S(1)}, u32[]{:S(2)}, u32[]{:S(2)}) collective-permute-start(f32[17,8,256]{2,1,0:T(8,128)} %get-tuple-element.14), channel_id=1, source_target_pairs={{1,2},{2,1},{3,4},{4,3},{5,6},{6,5},{7,8},{8,7},{9,10},{10,9},{11,... | collective-permute-start | bytes 417800 | tf_op jit(solution)/shard_map/ppermute | solution.py:534
  4.5 8.0 %collective-permute-start.1 = (f32[17,8,256]{2,1,0:T(8,128)}, f32[17,8,256]{2,1,0:T(8,128)S(1)}, u32[]{:S(2)}, u32[]{:S(2)}) collective-permute-start(f32[17,8,256]{2,1,0:T(8,128)} %get-tuple-element.15), channel_id=1, source_target_pairs={{0,1},{1,0},{2,3},{3,2},{4,5},{5,4},{6,7},{7,6},{8,9},{9,8},{10,11... | collective-permute-start | bytes 417800 | tf_op jit(solution)/shard_map/ppermute | solution.py:535
  12.6 6.4 %collective-permute-start.3 = (f32[192,128]{1,0:T(8,128)S(1)}, f32[192,128]{1,0:T(8,128)S(1)}, u32[]{:S(2)}, u32[]{:S(2)}) collective-permute-start(f32[192,128]{1,0:T(8,128)S(1)} %get-tuple-element.16.sent_even), channel_id=1, source_target_pairs={{0,16},{16,0},{32,48},{48,32},{64,80},{80,64},{96,112},{112,96},{1... | collective-permute-start | bytes 294920 | tf_op jit(solution)/shard_map/ppermute | solution.py:535
  14.2 4.8 %collective-permute-start.2 = (f32[192,128]{1,0:T(8,128)S(1)}, f32[192,128]{1,0:T(8,128)S(1)}, u32[]{:S(2)}, u32[]{:S(2)}) collective-permute-start(f32[192,128]{1,0:T(8,128)S(1)} %get-tuple-element.17.sent_odd), channel_id=1, source_target_pairs={{16,32},{32,16},{48,64},{64,48},{80,96},{96,80},{112,128},{128,112... | collective-permute-start | bytes 294920 | tf_op jit(solution)/shard_map/ppermute | solution.py:534
where the time goes:
time: 52.5 us; the launch traced here: 52.3 us
  blocking collectives  28.3 us (54%)
  Pallas kernels  12.6 us (24%)
  starting transfers between devices  8.67 us (17%)
  waiting for transfers between devices  1.96 us (4%)
  between operations  0.73 us (1%)
    all_to_all x1, blocking collectives, on_device(): shares = lax.all_to_all(shares, ('lon', 'lat'), 0, 0)  28.3 us
    ppermute x2, starting transfers between devices, exchange(): return (lax.ppermute(to_even, axis, even), from_odd)  6.38 us
    pallas_call x1, Pallas kernels, on_device(): pl.pallas_call(finish, in_specs=[vmem] * 6, out_specs=[hbm, vmem], out_sh...  3.24 us
    pallas_call x1, Pallas kernels, on_device(): pl.pallas_call(pack_rows, in_specs=[hbm] * 3, out_specs=[vmem] * 2, out_s...  3.16 us
    pallas_call x1, Pallas kernels, on_device(): pl.pallas_call(advance_inner, out_shape=[shape(2, levels, rows_here, brea...  3.13 us
    ppermute x2, starting transfers between devices, exchange(): from_odd = lax.ppermute(to_odd, axis, odd)  2.29 us
    ppermute x2, waiting for transfers between devices, exchange(): return (lax.ppermute(to_even, axis, even), from_odd)  1.95 us
    pallas_call x1, Pallas kernels, on_device(): pl.pallas_call(krylov, out_shape=[shape(2, 3, rows_here, LANES), shape(IT...  1.72 us
  transfers between devices with their start and end apart: 4, of which 1 were waited for; matrix products, arithmetic and copies ran while one was open for 0% of the time, Pallas kernels for 8%

commit v1 on v0

--- a/solution.py
+++ b/solution.py
@@ -220,7 +220,7 @@
     empty = jnp.zeros((2 * TILE, breadth), F32)
     blank = (jnp.zeros((2 * TILE, LANES), F32),) * 2
     sum_u, sum_v, strips_u, strips_v = lax.fori_loop(
-        0, levels, body, (empty, empty, blank, blank), unroll=2
+        0, levels, body, (empty, empty, blank, blank), unroll=4
     )
     starts = guess_ends[...]
     others = blank
@@ -450,15 +450,20 @@
 
     weighted = [inner(diagonal * x) for x in vectors] + [inner(last)]
     held = [inner(x) for x in vectors]
-    slot = lane_of((1, LANES))
-    total = jnp.zeros((1, LANES), F32)
+    slot = lane_of((TILE, LANES))
+    total = jnp.zeros((TILE, LANES), F32)
     for m in range(2 * ITERS):
         product = held[m // 2] * weighted[(m + 1) // 2]
-        total = jnp.where(slot == m, jnp.sum(product), total)
-    moments[...] = total
-
-
-def finish(shares, basis, edges, kmt, flow, tracer, out, pressure, done, sems):
+        folded = None
+        for i in range(0, rows_here, TILE):
+            for j in range(0, breadth, LANES):
+                part = product[i : i + TILE, j : j + LANES]
+                folded = part if folded is None else folded + part
+        total = jnp.where(slot == m, jnp.sum(folded, axis=1, keepdims=True), total)
+    moments[...] = jnp.sum(total, axis=0, keepdims=True)
+
+
+def finish(shares, basis, edges, kmt, flow, tracer, out, pressure, done, held, sems, held_sem):
     levels, rows_here, breadth = tracer.shape
     own = slice(TILE, TILE + rows_here)
     chunks = sems.shape[1]
@@ -482,10 +487,18 @@
         for k in range(c * size, (c + 1) * size):
             done[2, k] = ended(tracer[k], 2, k)
         send(2, 3, c).start()
-    sums = jnp.sum(shares[...], axis=0, keepdims=True)
-    res = [sums[:, m : m + 1] for m in range(2 * ITERS)]
+    totals = jnp.sum(shares[...].reshape(-1, TILE, LANES), axis=0)
+    for step in (1, 2, 4):
+        totals = totals + turn(totals, step, 0)
+    lane = lane_of((TILE, LANES))
+
+    def everywhere(m):
+        one = jnp.sum(jnp.where(lane == m, totals, 0.0), axis=1, keepdims=True)
+        return jnp.broadcast_to(one, (TILE, LANES))
+
+    res = [everywhere(m) for m in range(2 * ITERS)]
     dirn = list(res)
-    one, zero = (jnp.ones((1, 1), F32), jnp.zeros((1, 1), F32))
+    one, zero = (jnp.ones((TILE, LANES), F32), jnp.zeros((TILE, LANES), F32))
     res_in = [one] + [zero] * (ITERS - 1)
     dir_in = list(res_in)
     height_in = [zero] * ITERS
@@ -495,16 +508,31 @@
         height_in = [h + step * d for h, d in zip(height_in, dir_in)]
         if k + 1 < ITERS:
             new = [res[m] - step * (dirn[m] - dirn[m + 1]) for m in range(len(dirn) - 1)]
-            ratio = jnp.clip(step * new[k + 1] / res[k], 0.0, HIGHEST / LOWEST)
+            ratio = jnp.clip((step * (1.0 / res[k])) * new[k + 1], 0.0, HIGHEST / LOWEST)
             dirn = [n + ratio * d for n, d in zip(new, dirn)]
             res = new
             moved = [zero] + dir_in[:-1]
             res_in = [r - step * (d - m) for r, d, m in zip(res_in, dir_in, moved)]
             dir_in = [r + ratio * d for r, d in zip(res_in, dir_in)]
-    height = basis[0]
-    for k in range(ITERS):
-        height = height + height_in[k] * basis[k + 1]
-    pressure[...] = gravity * height[own, :breadth]
+
+    def tile_of(i, j):
+        cut = slice(i, i + TILE), slice(j, j + LANES)
+        value = basis[0, *cut]
+        for k in range(ITERS):
+            value = value + height_in[k] * basis[k + 1, *cut]
+        return value
+
+    tall, wide = basis.shape[1:]
+    height = jnp.concatenate(
+        [
+            jnp.concatenate([tile_of(i, j) for j in range(0, wide, LANES)], axis=1)
+            for i in range(0, tall, TILE)
+        ],
+        axis=0,
+    )
+    held[...] = gravity * height[own, :breadth]
+    pressure_out = pltpu.make_async_copy(held, pressure, held_sem.at[0])
+    pressure_out.start()
     pull = 0.5 * time_step * gravity
     slope_east = pull * (east_of(height) - west_of(height))[own, :breadth]
     slope_north = pull * (north_of(height) - south_of(height))[own, :breadth]
@@ -515,6 +543,7 @@
             for field, slope in ((0, slope_east), (1, slope_north)):
                 done[field, k] = jnp.where(wet, ended(flow[field, k], field, k) - slope, 0.0)
         send(0, 2, c).start()
+    pressure_out.wait()
     for c in range(chunks):
         send(2, 3, c).wait()
         send(0, 2, c).wait()
@@ -548,7 +577,7 @@
         pack_rows,
         in_specs=[hbm] * 3,
         out_specs=[vmem] * 2,
-        out_shape=[shape(SLOTS, TILE, breadth)] * 2,
+        out_shape=[pltpu.VMEM((SLOTS, TILE, breadth), F32)] * 2,
         scratch_shapes=[
             pltpu.VMEM((3, levels, 2 * TILE, breadth), F32),
             pltpu.VMEM((2 * TILE, breadth), jnp.int32),
@@ -604,11 +633,13 @@
     return pl.pallas_call(
         finish,
         in_specs=[vmem] * 6,
-        out_specs=[hbm, vmem],
+        out_specs=[hbm, hbm],
         out_shape=[shape(3, levels, rows_here, breadth), shape(rows_here, breadth)],
         scratch_shapes=[
             pltpu.VMEM((3, levels, rows_here, breadth), F32),
+            pltpu.VMEM((rows_here, breadth), F32),
             pltpu.SemaphoreType.DMA((2, 4)),
+            pltpu.SemaphoreType.DMA((1,)),
         ],
         compiler_params=params(),
     )(shares.reshape(devices, LANES), basis, edges, kmt, flow, tracer)

time: 52.5 us -> 49.6 us (0.945)
  Pallas kernels: 12.6 us -> 9.91 us
    pallas_call x1, Pallas kernels: 3.24 us -> 1.52 us  [on_device(): pl.pallas_call(finish, in_specs=[vmem] * 6, out_specs=[hbm, hbm], out_sha...]
    pallas_call x1, Pallas kernels: 3.16 us -> 2.26 us  [on_device(): pl.pallas_call(pack_rows, in_specs=[hbm] * 3, out_specs=[vmem] * 2, out_s...]
  transfers between devices with their start and end apart: 4 -> 4, of which waited for: 1 -> 1; matrix products, arithmetic and copies ran while one was open for 0% -> 0% of each run, Pallas kernels for 8% -> 9%
where the time goes in v1:
time: 49.6 us; the launch traced here: 49.5 us
  blocking collectives  28.3 us (57%)
  Pallas kernels  9.91 us (20%)
  starting transfers between devices  8.67 us (17%)
  waiting for transfers between devices  1.75 us (4%)
  between operations  0.72 us (1%)
    all_to_all x1, blocking collectives, on_device(): shares = lax.all_to_all(shares, ('lon', 'lat'), 0, 0)  28.3 us
    ppermute x2, starting transfers between devices, exchange(): return (lax.ppermute(to_even, axis, even), from_odd)  6.38 us
    pallas_call x1, Pallas kernels, on_device(): pl.pallas_call(advance_inner, out_shape=[shape(2, levels, rows_here, brea...  3.13 us
    ppermute x2, starting transfers between devices, exchange(): from_odd = lax.ppermute(to_odd, axis, odd)  2.29 us
    pallas_call x1, Pallas kernels, on_device(): pl.pallas_call(pack_rows, in_specs=[hbm] * 3, out_specs=[vmem] * 2, out_s...  2.26 us
    ppermute x2, waiting for transfers between devices, exchange(): return (lax.ppermute(to_even, axis, even), from_odd)  1.74 us
    pallas_call x1, Pallas kernels, on_device(): pl.pallas_call(krylov, out_shape=[shape(2, 3, rows_here, LANES), shape(IT...  1.68 us
    pallas_call x1, Pallas kernels, on_device(): pl.pallas_call(finish, in_specs=[vmem] * 6, out_specs=[hbm, hbm], out_sha...  1.52 us
  transfers between devices with their start and end apart: 4, of which 1 were waited for; matrix products, arithmetic and copies ran while one was open for 0% of the time, Pallas kernels for 9%

profile of v1, /device:TPU:1, one launch (start us, length us, event | category | flops | bytes accessed | tf_op | source)
XLA Modules:
  0.0 49.5 jit_solution(1953966598871848964)
XLA Ops:
  0.6 0.0 copy-start.1
  0.6 0.0 copy-start.2
  0.6 0.0 copy-start
  0.7 2.3 %shard_map.51 = (f32[17,8,256]{2,1,0:T(8,128)S(1)}, f32[17,8,256]{2,1,0:T(8,128)S(1)}) custom-call(f32[3,16,32,256]{3,2,1,0:T(8,128)} %state.5, s32[32,256]{1,0:T(8,128)} %kmt.9, f32[32,256]{1,0:T(8,128)} %guess.5), custom_call_target="tpu_custom_call" | custom-call | tf_op jit(solution)/shard_map/pallas_call | solution.py:576
  2.9 0.7 %collective-permute-start = (f32[17,8,256]{2,1,0:T(8,128)S(1)}, f32[17,8,256]{2,1,0:T(8,128)S(1)}, u32[]{:S(2)}, u32[]{:S(2)}) collective-permute-start(f32[17,8,256]{2,1,0:T(8,128)S(1)} %get-tuple-element.14), channel_id=1, source_target_pairs={{1,2},{2,1},{3,4},{4,3},{5,6},{6,5},{7,8},{8,7},{9,10},{10,9},{11,... | collective-permute-start | bytes 417800 | tf_op jit(solution)/shard_map/ppermute | solution.py:563
  3.6 4.7 %collective-permute-start.1 = (f32[17,8,256]{2,1,0:T(8,128)S(1)}, f32[17,8,256]{2,1,0:T(8,128)S(1)}, u32[]{:S(2)}, u32[]{:S(2)}) collective-permute-start(f32[17,8,256]{2,1,0:T(8,128)S(1)} %get-tuple-element.15), channel_id=1, source_target_pairs={{0,1},{1,0},{2,3},{3,2},{4,5},{5,4},{6,7},{7,6},{8,9},{9,8},{10,11... | collective-permute-start | bytes 417800 | tf_op jit(solution)/shard_map/ppermute | solution.py:564
  8.3 0.0 copy-done.1
  8.4 0.0 copy-done.2
  8.4 0.0 copy-done
  8.4 1.3 %shard_map.50.strips = f32[2,4,32,128]{3,2,1,0:T(8,128)S(1)} custom-call(f32[3,16,32,256]{3,2,1,0:T(8,128)S(1)} %copy-done, s32[32,256]{1,0:T(8,128)S(1)} %copy-done.1, f32[32,256]{1,0:T(8,128)S(1)} %copy-done.2), custom_call_target="tpu_custom_call" | custom-call | flops 23592960 | bytes 3145728 | tf_op jit(solution)/shard_map/pallas_call | solution.py:591
  9.7 0.0 collective-permute-done.rows_odd
  9.7 1.7 %collective-permute-done.1.rows_even = f32[17,8,256]{2,1,0:T(8,128)S(1)} collective-permute-done((f32[17,8,256]{2,1,0:T(8,128)S(1)}, f32[17,8,256]{2,1,0:T(8,128)S(1)}, u32[]{:S(2)}, u32[]{:S(2)}) %collective-permute-start.1) | collective-permute-done | bytes 139296 | tf_op jit(solution)/shard_map/ppermute | solution.py:564
  11.5 1.6 %collective-permute-start.3 = (f32[192,128]{1,0:T(8,128)S(1)}, f32[192,128]{1,0:T(8,128)S(1)}, u32[]{:S(2)}, u32[]{:S(2)}) collective-permute-start(f32[192,128]{1,0:T(8,128)S(1)} %get-tuple-element.16.sent_even), channel_id=1, source_target_pairs={{0,16},{16,0},{32,48},{48,32},{64,80},{80,64},{96,112},{112,96},{1... | collective-permute-start | bytes 294920 | tf_op jit(solution)/shard_map/ppermute | solution.py:564
  13.1 1.6 %collective-permute-start.2 = (f32[192,128]{1,0:T(8,128)S(1)}, f32[192,128]{1,0:T(8,128)S(1)}, u32[]{:S(2)}, u32[]{:S(2)}) collective-permute-start(f32[192,128]{1,0:T(8,128)S(1)} %get-tuple-element.17.sent_odd), channel_id=1, source_target_pairs={{16,32},{32,16},{48,64},{64,48},{80,96},{96,80},{112,128},{128,112... | collective-permute-start | bytes 294920 | tf_op jit(solution)/shard_map/ppermute | solution.py:563
  14.7 3.1 %shard_map.53 = (f32[2,16,32,256]{3,2,1,0:T(8,128)S(1)}, f32[16,32,256]{2,1,0:T(8,128)S(1)}, f32[48,256]{1,0:T(8,128)S(1)}, f32[48,256]{1,0:T(8,128)S(1)}, f32[48,128]{1,0:T(8,128)S(1)}) custom-call(f32[3,16,32,256]{3,2,1,0:T(8,128)S(1)} %copy-done, s32[32,256]{1,0:T(8,128)S(1)} %copy-done.1, f32[17,8,256]{2,1,0:T(8,128)S(1)} %collective-permute-done.rows_odd, ...), custom_call_target="tpu_custom_call" | custom-call | flops 23592960 | bytes 3145728 | tf_op jit(solution)/shard_map/pallas_call | solution.py:605
  17.8 0.0 collective-permute-done.3.got_even
  17.9 0.0 collective-permute-done.2.got_odd
  17.9 1.7 %shard_map.54 = (f32[2,3,32,128]{3,2,1,0:T(8,128)S(1)}, f32[5,48,384]{2,1,0:T(8,128)S(1)}, f32[1,128]{1,0:T(1,128)S(1)}) custom-call(f32[192,128]{1,0:T(8,128)S(1)} %get-tuple-element.16.sent_even, f32[192,128]{1,0:T(8,128)S(1)} %get-tuple-element.17.sent_odd, f32[192,128]{1,0:T(8,128)S(1)} %collective-permute-done.2.got_odd, ...), custom_call_target="tpu_custom_call" | custom-call | tf_op jit(solution)/shard_map/pallas_call | solution.py:618
  19.5 0.1 broadcast_in_dim.9
  19.6 28.3 %all_to_all.5 = f32[256,1,128]{2,1,0:T(1,128)S(1)} all-to-all(f32[256,1,128]{2,1,0:T(1,128)S(1)} %broadcast_in_dim.9), channel_id=1, replica_groups=mesh['lon'=16,'lat'=16] {'lon','lat'}, dimensions={0} | all-to-all | bytes 262144 | tf_op jit(solution)/shard_map/all_to_all | solution.py:632
  47.9 1.5 %shard_map.55 = (f32[3,16,32,256]{3,2,1,0:T(8,128)}, f32[32,256]{1,0:T(8,128)}) custom-call(f32[256,128]{1,0:T(8,128)S(1)} %bitcast.2, f32[5,48,384]{2,1,0:T(8,128)S(1)} %get-tuple-element.22.basis, f32[2,3,32,128]{3,2,1,0:T(8,128)S(1)} %get-tuple-element.23.edges, s32[32,256]{1,0:T(8,128)S(1)} %copy-done.1, f32[2,16,32,256]{3,2,1,0:T(8,128)S(1)} %get-tuple-element.24.flow, ...), custom_call_target="tpu_custom_call" | custom-call | tf_op jit(solution)/shard_map/pallas_call | solution.py:633
  (1 shorter events, 0.0 us)
Async XLA Ops:
  0.6 7.7 %copy-start.1 = (s32[32,256]{1,0:T(8,128)S(1)}, s32[32,256]{1,0:T(8,128)}, u32[]{:S(2)}) copy-start(s32[32,256]{1,0:T(8,128)} %kmt.9) | copy-start | bytes 98308
  0.6 7.7 %copy-start.2 = (f32[32,256]{1,0:T(8,128)S(1)}, f32[32,256]{1,0:T(8,128)}, u32[]{:S(2)}) copy-start(f32[32,256]{1,0:T(8,128)} %guess.5) | copy-start | bytes 98308
  0.6 7.7 %copy-start = (f32[3,16,32,256]{3,2,1,0:T(8,128)S(1)}, f32[3,16,32,256]{3,2,1,0:T(8,128)}, u32[]{:S(2)}) copy-start(f32[3,16,32,256]{3,2,1,0:T(8,128)} %state.5) | copy-start | bytes 4718596
  2.9 6.8 %collective-permute-start = (f32[17,8,256]{2,1,0:T(8,128)S(1)}, f32[17,8,256]{2,1,0:T(8,128)S(1)}, u32[]{:S(2)}, u32[]{:S(2)}) collective-permute-start(f32[17,8,256]{2,1,0:T(8,128)S(1)} %get-tuple-element.14), channel_id=1, source_target_pairs={{1,2},{2,1},{3,4},{4,3},{5,6},{6,5},{7,8},{8,7},{9,10},{10,9},{11,... | collective-permute-start | bytes 417800 | tf_op jit(solution)/shard_map/ppermute | solution.py:563
  3.6 7.8 %collective-permute-start.1 = (f32[17,8,256]{2,1,0:T(8,128)S(1)}, f32[17,8,256]{2,1,0:T(8,128)S(1)}, u32[]{:S(2)}, u32[]{:S(2)}) collective-permute-start(f32[17,8,256]{2,1,0:T(8,128)S(1)} %get-tuple-element.15), channel_id=1, source_target_pairs={{0,1},{1,0},{2,3},{3,2},{4,5},{5,4},{6,7},{7,6},{8,9},{9,8},{10,11... | collective-permute-start | bytes 417800 | tf_op jit(solution)/shard_map/ppermute | solution.py:564
  11.5 6.4 %collective-permute-start.3 = (f32[192,128]{1,0:T(8,128)S(1)}, f32[192,128]{1,0:T(8,128)S(1)}, u32[]{:S(2)}, u32[]{:S(2)}) collective-permute-start(f32[192,128]{1,0:T(8,128)S(1)} %get-tuple-element.16.sent_even), channel_id=1, source_target_pairs={{0,16},{16,0},{32,48},{48,32},{64,80},{80,64},{96,112},{112,96},{1... | collective-permute-start | bytes 294920 | tf_op jit(solution)/shard_map/ppermute | solution.py:564
  13.1 4.8 %collective-permute-start.2 = (f32[192,128]{1,0:T(8,128)S(1)}, f32[192,128]{1,0:T(8,128)S(1)}, u32[]{:S(2)}, u32[]{:S(2)}) collective-permute-start(f32[192,128]{1,0:T(8,128)S(1)} %get-tuple-element.17.sent_odd), channel_id=1, source_target_pairs={{16,32},{32,16},{48,64},{64,48},{80,96},{96,80},{112,128},{128,112... | collective-permute-start | bytes 294920 | tf_op jit(solution)/shard_map/ppermute | solution.py:563

commit v2 on v1

--- a/solution.py
+++ b/solution.py
@@ -27,7 +27,7 @@
 U_ROWS = 0
 V_ROWS = U_ROWS + LEVELS // 4
 T_ROWS = V_ROWS + LEVELS // 4
-KMT, GUESS, SUM_U, SUM_V, STRIPS = range(T_ROWS + LEVELS // 8, T_ROWS + LEVELS // 8 + 5)
+KMT, GUESS, SUMS, STRIPS = range(T_ROWS + LEVELS // 8, T_ROWS + LEVELS // 8 + 4)
 SLOTS = STRIPS + 3
 
 LOWEST = storage / (storage + 4 * edge_weight + 4 * corner_weight)
@@ -102,6 +102,9 @@
 
         acc = lax.fori_loop(0, levels, body, blank, unroll=4)
         strips[0, field], strips[1, field] = acc
+    slot = lax.rem(lane_of((rows_here, LANES)), TILE)
+    strips[0, 0] = jnp.where(slot == 1, turn(strips[0, 2], -1, 1), strips[0, 0])
+    strips[1, 0] = jnp.where(slot == HALO, turn(strips[1, 2], 1, 1), strips[1, 0])
     acc = blank
     for number, own in enumerate((kmt[...].astype(F32), guess[...])):
         west, east = [own[:, cols] for cols in ends]
@@ -109,21 +112,24 @@
     strips[0, 3], strips[1, 3] = acc
 
 
-def pack_cols(strips, rows_odd, rows_even, msg_odd, msg_even):
+def pack_cols(strips, rows_odd, rows_even, msg_odd, msg_even, own_tracer):
     tall = strips.shape[2] + 2 * TILE
     lat_even = is_even("lat")
     lon_even = is_even("lon")
 
-    def put(number, field, south, north):
-        base = number * tall
-        to_west, to_east = (
+    def tall_strips(field, south, north):
+        return [
             stacked(
                 south[:, i * LANES : (i + 1) * LANES],
                 strips[i, field],
                 north[:, i * LANES : (i + 1) * LANES],
             )
             for i in range(2)
-        )
+        ]
+
+    def put(number, field, south, north):
+        base = number * tall
+        to_west, to_east = tall_strips(field, south, north)
         a, b = swap(lon_even, to_east, to_west)
         msg_even[base : base + tall] = a
         msg_odd[base : base + tall] = b
@@ -135,7 +141,9 @@
     put(0, 0, *halos[0])
     put(1, 1, *halos[1])
     put(2, 3, *halos[2])
-    put(3, 2, turn(halos[0][0], -1, 0), turn(halos[0][1], 1, 0))
+    own_tracer[0], own_tracer[1] = tall_strips(
+        2, turn(halos[0][0], -1, 0), turn(halos[0][1], 1, 0)
+    )
 
 
 def rotation_at(row, rows_here):
@@ -177,26 +185,38 @@
     return jnp.where(wet, new_u, 0.0), jnp.where(wet, new_v, 0.0)
 
 
+def is_sum_u(row, southern):
+    first = TILE - 5 if southern else 1
+    return (row >= first) & (row < first + 4)
+
+
 def pack_rows(state, kmt, guess, msg_odd, msg_even, ends, wet_ends, guess_ends, sems):
     levels, rows_here, breadth = state.shape[1:]
     even = is_even("lat")
+    parts = [slice(k, k + levels // 4) for k in range(0, levels, levels // 4)]
     copies = []
-    for number, rows in enumerate((slice(0, TILE), slice(rows_here - TILE, rows_here))):
-        held = slice(number * TILE, (number + 1) * TILE)
-        for source, target in (
-            (state.at[:, :, rows, :], ends.at[:, :, held, :]),
-            (kmt.at[rows, :], wet_ends.at[held, :]),
-            (guess.at[rows, :], guess_ends.at[held, :]),
-        ):
-            copies.append(pltpu.make_async_copy(source, target, sems.at[len(copies)]))
-            copies[-1].start()
+    for part in [None] + parts:
+        copies.append([])
+        for number, rows in enumerate((slice(0, TILE), slice(rows_here - TILE, rows_here))):
+            held = slice(number * TILE, (number + 1) * TILE)
+            if part is not None:
+                pairs_of_refs = [(state.at[:, part, rows, :], ends.at[:, part, held, :])]
+            else:
+                pairs_of_refs = [
+                    (kmt.at[rows, :], wet_ends.at[held, :]),
+                    (guess.at[rows, :], guess_ends.at[held, :]),
+                ]
+            for source, target in pairs_of_refs:
+                item = pltpu.make_async_copy(source, target, sems.at[sum(map(len, copies))])
+                item.start()
+                copies[-1].append(item)
     row = lax.broadcasted_iota(jnp.int32, (2 * TILE, LANES), 0)
     rotation = rotation_at(jnp.where(row < TILE, row, row + rows_here - 2 * TILE), rows_here)
     half_turn = time_step * rotation[:, :1]
     group = lane_of((2 * TILE, LANES)) // TILE
     row = lax.broadcasted_iota(jnp.int32, (2 * TILE, breadth), 0)
     borrowed = (row == TILE - 1) | (row == TILE)
-    for item in copies:
+    for item in copies[0]:
         item.wait()
 
     depth = wet_ends[...].astype(F32)
@@ -219,9 +239,12 @@
 
     empty = jnp.zeros((2 * TILE, breadth), F32)
     blank = (jnp.zeros((2 * TILE, LANES), F32),) * 2
-    sum_u, sum_v, strips_u, strips_v = lax.fori_loop(
-        0, levels, body, (empty, empty, blank, blank), unroll=4
-    )
+    carried = (empty, empty, blank, blank)
+    for part, items in zip(parts, copies[1:]):
+        for item in items:
+            item.wait()
+        carried = lax.fori_loop(part.start, part.stop, body, carried, unroll=4)
+    sum_u, sum_v, strips_u, strips_v = carried
     starts = guess_ends[...]
     others = blank
     for number, value in enumerate((depth, starts)):
@@ -232,7 +255,12 @@
         msg_even[slot] = a
         msg_odd[slot] = b
 
-    whole = [depth, starts, sum_u, sum_v]
+    row = lax.rem(lax.broadcasted_iota(jnp.int32, (2 * TILE, breadth), 0), TILE)
+    first = jnp.concatenate(
+        [is_sum_u(row[:TILE], False), is_sum_u(row[TILE:], True)], axis=0
+    )
+    moved = jnp.concatenate([turn(sum_v[:TILE], 4, 0), turn(sum_v[TILE:], 4, 0)], axis=0)
+    whole = [depth, starts, jnp.where(first, sum_u, moved)]
     whole += [jnp.concatenate(pair, axis=1) for pair in (strips_u, strips_v, others)]
     for slot, value in enumerate(whole, KMT):
         put(slot, value[:TILE], value[TILE:])
@@ -312,8 +340,9 @@
     row = lax.broadcasted_iota(jnp.int32, (tall, breadth), 0)
     outer = (row < TILE - 1) | (row > TILE + rows_here)
     inner = jnp.zeros((rows_here, breadth), F32)
-    for slot, flow_sum in ((SUM_U, flow_u), (SUM_V, flow_v)):
-        south, north = halos(slot)
+    sums = halos(SUMS)
+    for shift, flow_sum in ((0, flow_u), (-4, flow_v)):
+        south, north = [turn(x, shift, 0) for x in sums]
         flow_sum[...] = jnp.where(outer, stacked(south, inner, north), flow_sum[...])
 
 
@@ -339,7 +368,7 @@
 
 def krylov(
     sent_even, sent_odd, got_odd, got_even, flow_u, flow_v, kmt, guess,
-    rows_even, rows_odd, turning, edges, basis, moments,
+    rows_even, rows_odd, turning, own_tracer, edges, basis, moments,
 ):
     levels = LEVELS
     rows_here, breadth = kmt.shape
@@ -353,20 +382,28 @@
     own = slice(TILE, TILE + rows_here)
     half_turn = time_step * turning[...]
 
+    def received(slot):
+        rows = slice(slot * tall, (slot + 1) * tall)
+        from_east, from_west = swap(lon_even, got_even[rows], got_odd[rows])
+        return from_west, from_east
+
     def strips(slot):
         rows = slice(slot * tall, (slot + 1) * tall)
         to_east, to_west = swap(lon_even, sent_even[rows], sent_odd[rows])
-        from_east, from_west = swap(lon_even, got_even[rows], got_odd[rows])
+        from_west, from_east = received(slot)
         west = jnp.where(place < HALO, from_west, turn(to_west, 4, 1))
         east = jnp.where(place >= TILE - HALO, from_east, turn(to_east, -4, 1))
         return west, east
 
     u_sides, v_sides, other = [strips(slot) for slot in range(3)]
-    t_sides = strips(3)
+    from_west, from_east = received(0)
+    t_sides = (
+        jnp.where(place == HALO - 1, turn(from_west, -1, 1), turn(own_tracer[0], 4, 1)),
+        jnp.where(place == TILE - HALO, turn(from_east, 1, 1), turn(own_tracer[1], -4, 1)),
+    )
     sums = []
     for side in range(2):
         depth = over_groups(jnp.where(group == 0, other[side], 0.0))
-        start = over_groups(jnp.where(group == 1, other[side], 0.0))
         wet = depth > level
         count = count_wet(around(depth), level)
         u = jnp.where(wet, u_sides[side], 0.0)
@@ -382,10 +419,10 @@
         edges[side, 0] = new_u[own]
         edges[side, 1] = new_v[own]
         edges[side, 2] = new_t[own]
-        sums.append((over_groups(new_u), over_groups(new_v), depth, start))
+        sums.append((over_groups(new_u), over_groups(new_v), depth, turn(other[side], -TILE, 1)))
 
     def assemble(field, number, seam):
-        west = turn(sums[0][number], 2, 1)
+        west = turn(sums[0][number], -HALO, 1)
         east = turn(sums[1][number], -2, 1)
         halo = jnp.where(lane < LANES // 2, east, west)
         tiles = [field[:, i : i + LANES] for i in range(0, breadth, LANES)]
@@ -582,7 +619,7 @@
             pltpu.VMEM((3, levels, 2 * TILE, breadth), F32),
             pltpu.VMEM((2 * TILE, breadth), jnp.int32),
             pltpu.VMEM((2 * TILE, breadth), F32),
-            pltpu.SemaphoreType.DMA((6,)),
+            pltpu.SemaphoreType.DMA((12,)),
         ],
         compiler_params=params(VMEM_FIRST),
     )(state, kmt, first_guess)
@@ -594,10 +631,10 @@
         compiler_params=params(),
         cost_estimate=cost(state.size),
     )(state, kmt, first_guess)
-    length = 4 * tall
-    sent_odd, sent_even = pl.pallas_call(
+    length = 3 * tall
+    sent_odd, sent_even, own_tracer = pl.pallas_call(
         pack_cols,
-        out_shape=[shape(length, LANES)] * 2,
+        out_shape=[shape(length, LANES)] * 2 + [shape(2, tall, LANES)],
         compiler_params=params(),
     )(strips, rows_odd, rows_even)
     got_even, got_odd = exchange("lon", sent_even, sent_odd)
@@ -625,7 +662,7 @@
         compiler_params=params(),
     )(
         sent_even, sent_odd, got_odd, got_even, flow_u, flow_v, kmt, first_guess,
-        rows_even, rows_odd, turning,
+        rows_even, rows_odd, turning, own_tracer,
     )
 
     shares = jnp.broadcast_to(moments[None], (devices, 1, LANES))

time: 49.6 us -> 48.9 us (0.986)
  no operation moved by 1% of the time
where the time goes in v2:
time: 48.9 us; the launch traced here: 48.8 us
  blocking collectives  28.1 us (57%)
  Pallas kernels  9.64 us (20%)
  starting transfers between devices  8.67 us (18%)
  waiting for transfers between devices  1.56 us (3%)
  between operations  0.73 us (1%)
    all_to_all x1, blocking collectives, on_device(): shares = lax.all_to_all(shares, ('lon', 'lat'), 0, 0)  28.1 us
    ppermute x2, starting transfers between devices, exchange(): return (lax.ppermute(to_even, axis, even), from_odd)  6.38 us
    pallas_call x1, Pallas kernels, on_device(): pl.pallas_call(advance_inner, out_shape=[shape(2, levels, rows_here, brea...  3.1 us
    ppermute x2, starting transfers between devices, exchange(): from_odd = lax.ppermute(to_odd, axis, odd)  2.29 us
    pallas_call x1, Pallas kernels, on_device(): pl.pallas_call(pack_rows, in_specs=[hbm] * 3, out_specs=[vmem] * 2, out_s...  2.02 us
    pallas_call x1, Pallas kernels, on_device(): pl.pallas_call(krylov, out_shape=[shape(2, 3, rows_here, LANES), shape(IT...  1.67 us
    ppermute x2, waiting for transfers between devices, exchange(): return (lax.ppermute(to_even, axis, even), from_odd)  1.56 us
    pallas_call x1, Pallas kernels, on_device(): pl.pallas_call(finish, in_specs=[vmem] * 6, out_specs=[hbm, hbm], out_sha...  1.52 us
  transfers between devices with their start and end apart: 4, of which 1 were waited for; matrix products, arithmetic and copies ran while one was open for 0% of the time, Pallas kernels for 9%

profile of v2, /device:TPU:1, one launch (start us, length us, event | category | flops | bytes accessed | tf_op | source)
XLA Modules:
  0.0 48.8 jit_solution(10444727441834083497)
XLA Ops:
  0.6 0.0 copy-start.1
  0.6 0.0 copy-start.2
  0.6 0.0 copy-start
  0.7 2.0 %shard_map.51 = (f32[16,8,256]{2,1,0:T(8,128)S(1)}, f32[16,8,256]{2,1,0:T(8,128)S(1)}) custom-call(f32[3,16,32,256]{3,2,1,0:T(8,128)} %state.5, s32[32,256]{1,0:T(8,128)} %kmt.9, f32[32,256]{1,0:T(8,128)} %guess.5), custom_call_target="tpu_custom_call" | custom-call | tf_op jit(solution)/shard_map/pallas_call | solution.py:613
  2.7 0.7 %collective-permute-start = (f32[16,8,256]{2,1,0:T(8,128)S(1)}, f32[16,8,256]{2,1,0:T(8,128)S(1)}, u32[]{:S(2)}, u32[]{:S(2)}) collective-permute-start(f32[16,8,256]{2,1,0:T(8,128)S(1)} %get-tuple-element.15), channel_id=1, source_target_pairs={{1,2},{2,1},{3,4},{4,3},{5,6},{6,5},{7,8},{8,7},{9,10},{10,9},{11,... | collective-permute-start | bytes 393224 | tf_op jit(solution)/shard_map/ppermute | solution.py:600
  3.4 4.7 %collective-permute-start.1 = (f32[16,8,256]{2,1,0:T(8,128)S(1)}, f32[16,8,256]{2,1,0:T(8,128)S(1)}, u32[]{:S(2)}, u32[]{:S(2)}) collective-permute-start(f32[16,8,256]{2,1,0:T(8,128)S(1)} %get-tuple-element.16), channel_id=1, source_target_pairs={{0,1},{1,0},{2,3},{3,2},{4,5},{5,4},{6,7},{7,6},{8,9},{9,8},{10,11... | collective-permute-start | bytes 393224 | tf_op jit(solution)/shard_map/ppermute | solution.py:601
  8.1 0.0 copy-done.1
  8.1 0.0 copy-done.2
  8.1 0.0 copy-done
  8.1 1.3 %shard_map.50.strips = f32[2,4,32,128]{3,2,1,0:T(8,128)S(1)} custom-call(f32[3,16,32,256]{3,2,1,0:T(8,128)S(1)} %copy-done, s32[32,256]{1,0:T(8,128)S(1)} %copy-done.1, f32[32,256]{1,0:T(8,128)S(1)} %copy-done.2), custom_call_target="tpu_custom_call" | custom-call | flops 23592960 | bytes 3145728 | tf_op jit(solution)/shard_map/pallas_call | solution.py:628
  9.4 0.0 collective-permute-done.rows_odd
  9.5 1.6 %collective-permute-done.1.rows_even = f32[16,8,256]{2,1,0:T(8,128)S(1)} collective-permute-done((f32[16,8,256]{2,1,0:T(8,128)S(1)}, f32[16,8,256]{2,1,0:T(8,128)S(1)}, u32[]{:S(2)}, u32[]{:S(2)}) %collective-permute-start.1) | collective-permute-done | bytes 131104 | tf_op jit(solution)/shard_map/ppermute | solution.py:601
  11.0 1.6 %collective-permute-start.3 = (f32[144,128]{1,0:T(8,128)S(1)}, f32[144,128]{1,0:T(8,128)S(1)}, u32[]{:S(2)}, u32[]{:S(2)}) collective-permute-start(f32[144,128]{1,0:T(8,128)S(1)} %get-tuple-element.17.sent_even), channel_id=1, source_target_pairs={{0,16},{16,0},{32,48},{48,32},{64,80},{80,64},{96,112},{112,96},{1... | collective-permute-start | bytes 221192 | tf_op jit(solution)/shard_map/ppermute | solution.py:601
  12.7 1.6 %collective-permute-start.2 = (f32[144,128]{1,0:T(8,128)S(1)}, f32[144,128]{1,0:T(8,128)S(1)}, u32[]{:S(2)}, u32[]{:S(2)}) collective-permute-start(f32[144,128]{1,0:T(8,128)S(1)} %get-tuple-element.18.sent_odd), channel_id=1, source_target_pairs={{16,32},{32,16},{48,64},{64,48},{80,96},{96,80},{112,128},{128,112... | collective-permute-start | bytes 221192 | tf_op jit(solution)/shard_map/ppermute | solution.py:600
  14.3 3.1 %shard_map.53 = (f32[2,16,32,256]{3,2,1,0:T(8,128)S(1)}, f32[16,32,256]{2,1,0:T(8,128)S(1)}, f32[48,256]{1,0:T(8,128)S(1)}, f32[48,256]{1,0:T(8,128)S(1)}, f32[48,128]{1,0:T(8,128)S(1)}) custom-call(f32[3,16,32,256]{3,2,1,0:T(8,128)S(1)} %copy-done, s32[32,256]{1,0:T(8,128)S(1)} %copy-done.1, f32[16,8,256]{2,1,0:T(8,128)S(1)} %collective-permute-done.rows_odd, ...), custom_call_target="tpu_custom_call" | custom-call | flops 23592960 | bytes 3145728 | tf_op jit(solution)/shard_map/pallas_call | solution.py:642
  17.4 0.0 collective-permute-done.3.got_even
  17.4 0.0 collective-permute-done.2.got_odd
  17.4 1.7 %shard_map.54 = (f32[2,3,32,128]{3,2,1,0:T(8,128)S(1)}, f32[5,48,384]{2,1,0:T(8,128)S(1)}, f32[1,128]{1,0:T(1,128)S(1)}) custom-call(f32[144,128]{1,0:T(8,128)S(1)} %get-tuple-element.17.sent_even, f32[144,128]{1,0:T(8,128)S(1)} %get-tuple-element.18.sent_odd, f32[144,128]{1,0:T(8,128)S(1)} %collective-permute-done.2.got_odd, ...), custom_call_target="tpu_custom_call" | custom-call | tf_op jit(solution)/shard_map/pallas_call | solution.py:655
  19.1 0.1 broadcast_in_dim.9
  19.2 28.1 %all_to_all.5 = f32[256,1,128]{2,1,0:T(1,128)S(1)} all-to-all(f32[256,1,128]{2,1,0:T(1,128)S(1)} %broadcast_in_dim.9), channel_id=1, replica_groups=mesh['lon'=16,'lat'=16] {'lon','lat'}, dimensions={0} | all-to-all | bytes 262144 | tf_op jit(solution)/shard_map/all_to_all | solution.py:669
  47.2 1.5 %shard_map.55 = (f32[3,16,32,256]{3,2,1,0:T(8,128)}, f32[32,256]{1,0:T(8,128)}) custom-call(f32[256,128]{1,0:T(8,128)S(1)} %bitcast.2, f32[5,48,384]{2,1,0:T(8,128)S(1)} %get-tuple-element.24.basis, f32[2,3,32,128]{3,2,1,0:T(8,128)S(1)} %get-tuple-element.25.edges, s32[32,256]{1,0:T(8,128)S(1)} %copy-done.1, f32[2,16,32,256]{3,2,1,0:T(8,128)S(1)} %get-tuple-element.26.flow, ...), custom_call_target="tpu_custom_call" | custom-call | tf_op jit(solution)/shard_map/pallas_call | solution.py:670
  (1 shorter events, 0.0 us)
Async XLA Ops:
  0.6 7.5 %copy-start.1 = (s32[32,256]{1,0:T(8,128)S(1)}, s32[32,256]{1,0:T(8,128)}, u32[]{:S(2)}) copy-start(s32[32,256]{1,0:T(8,128)} %kmt.9) | copy-start | bytes 98308
  0.6 7.5 %copy-start.2 = (f32[32,256]{1,0:T(8,128)S(1)}, f32[32,256]{1,0:T(8,128)}, u32[]{:S(2)}) copy-start(f32[32,256]{1,0:T(8,128)} %guess.5) | copy-start | bytes 98308
  0.6 7.5 %copy-start = (f32[3,16,32,256]{3,2,1,0:T(8,128)S(1)}, f32[3,16,32,256]{3,2,1,0:T(8,128)}, u32[]{:S(2)}) copy-start(f32[3,16,32,256]{3,2,1,0:T(8,128)} %state.5) | copy-start | bytes 4718596
  2.7 6.8 %collective-permute-start = (f32[16,8,256]{2,1,0:T(8,128)S(1)}, f32[16,8,256]{2,1,0:T(8,128)S(1)}, u32[]{:S(2)}, u32[]{:S(2)}) collective-permute-start(f32[16,8,256]{2,1,0:T(8,128)S(1)} %get-tuple-element.15), channel_id=1, source_target_pairs={{1,2},{2,1},{3,4},{4,3},{5,6},{6,5},{7,8},{8,7},{9,10},{10,9},{11,... | collective-permute-start | bytes 393224 | tf_op jit(solution)/shard_map/ppermute | solution.py:600
  3.4 7.7 %collective-permute-start.1 = (f32[16,8,256]{2,1,0:T(8,128)S(1)}, f32[16,8,256]{2,1,0:T(8,128)S(1)}, u32[]{:S(2)}, u32[]{:S(2)}) collective-permute-start(f32[16,8,256]{2,1,0:T(8,128)S(1)} %get-tuple-element.16), channel_id=1, source_target_pairs={{0,1},{1,0},{2,3},{3,2},{4,5},{5,4},{6,7},{7,6},{8,9},{9,8},{10,11... | collective-permute-start | bytes 393224 | tf_op jit(solution)/shard_map/ppermute | solution.py:601
  11.0 6.4 %collective-permute-start.3 = (f32[144,128]{1,0:T(8,128)S(1)}, f32[144,128]{1,0:T(8,128)S(1)}, u32[]{:S(2)}, u32[]{:S(2)}) collective-permute-start(f32[144,128]{1,0:T(8,128)S(1)} %get-tuple-element.17.sent_even), channel_id=1, source_target_pairs={{0,16},{16,0},{32,48},{48,32},{64,80},{80,64},{96,112},{112,96},{1... | collective-permute-start | bytes 221192 | tf_op jit(solution)/shard_map/ppermute | solution.py:601
  12.7 4.7 %collective-permute-start.2 = (f32[144,128]{1,0:T(8,128)S(1)}, f32[144,128]{1,0:T(8,128)S(1)}, u32[]{:S(2)}, u32[]{:S(2)}) collective-permute-start(f32[144,128]{1,0:T(8,128)S(1)} %get-tuple-element.18.sent_odd), channel_id=1, source_target_pairs={{16,32},{32,16},{48,64},{64,48},{80,96},{96,80},{112,128},{128,112... | collective-permute-start | bytes 221192 | tf_op jit(solution)/shard_map/ppermute | solution.py:600

commit v3 on v2

--- a/solution.py
+++ b/solution.py
@@ -25,9 +25,9 @@
 HALO = 6
 
 U_ROWS = 0
-V_ROWS = U_ROWS + LEVELS // 4
-T_ROWS = V_ROWS + LEVELS // 4
-KMT, GUESS, SUMS, STRIPS = range(T_ROWS + LEVELS // 8, T_ROWS + LEVELS // 8 + 4)
+V_ROWS = U_ROWS + LEVELS // TILE
+T_ROWS = V_ROWS + LEVELS // TILE
+KMT, GUESS, SUMS, STRIPS = range(T_ROWS + LEVELS // TILE, T_ROWS + LEVELS // TILE + 4)
 SLOTS = STRIPS + 3
 
 LOWEST = storage / (storage + 4 * edge_weight + 4 * corner_weight)
@@ -87,6 +87,19 @@
         group == k, pltpu.roll(east, lax.rem(HALO + TILE * k, LANES), 1), to_east
     )
     return to_west, to_east
+
+
+def over_groups(x):
+    for step in (TILE, 2 * TILE, 4 * TILE, 8 * TILE):
+        x = x + pltpu.roll(x, step, 1)
+    return x
+
+
+def pack_others(group, wet, guess, cut):
+    blank = (jnp.zeros_like(wet[:, cut[0]]),) * 2
+    wet = place(group, jnp.int32(0), wet[:, cut[0]], wet[:, cut[1]], blank)
+    wet = tuple(over_groups(x) for x in wet)
+    return place(group, jnp.int32(1), guess[:, cut[0]], guess[:, cut[1]], wet)
 
 
 def pack_own(state, kmt, guess, strips):
@@ -105,11 +118,7 @@
     slot = lax.rem(lane_of((rows_here, LANES)), TILE)
     strips[0, 0] = jnp.where(slot == 1, turn(strips[0, 2], -1, 1), strips[0, 0])
     strips[1, 0] = jnp.where(slot == HALO, turn(strips[1, 2], 1, 1), strips[1, 0])
-    acc = blank
-    for number, own in enumerate((kmt[...].astype(F32), guess[...])):
-        west, east = [own[:, cols] for cols in ends]
-        acc = place(group, jnp.int32(number), west, east, acc)
-    strips[0, 3], strips[1, 3] = acc
+    strips[0, 3], strips[1, 3] = pack_others(group, kmt[...].astype(F32), guess[...], ends)
 
 
 def pack_cols(strips, rows_odd, rows_even, msg_odd, msg_even, own_tracer):
@@ -178,7 +187,7 @@
 carry = 0.5 * time_step * advection_scale
 
 
-def advance_flow(u, v, wet, count, half_turn):
+def advance_flow(u, v, wet, count, half_turn, around=around):
     zonal, merid = (carry * u, carry * v)
     new_u = u + (spread(u, around(u), count, viscosity, zonal, merid) + half_turn * v)
     new_v = v + (spread(v, around(v), count, viscosity, zonal, merid) - half_turn * u)
@@ -219,9 +228,17 @@
     for item in copies[0]:
         item.wait()
 
+    top = row == 2 * TILE - 1
+
+    def within(x):
+        east, west, north, south = around(x)
+        return east, west, jnp.where(top, 0.0, north), jnp.where(row == 0, 0.0, south)
+
     depth = wet_ends[...].astype(F32)
-    beside = around(depth)
+    beside = within(depth)
     cut = slice(0, LANES), slice(breadth - LANES, breadth)
+    starts = guess_ends[...]
+    others = pack_others(group, depth, starts, cut)
 
     def body(k, carried):
         sum_u, sum_v, strips_u, strips_v = carried
@@ -230,7 +247,9 @@
         raw_u, raw_v, raw_t = [ends[field, k] for field in range(3)]
         u = jnp.where(wet, raw_u, 0.0)
         v = jnp.where(wet, raw_v, 0.0)
-        new_u, new_v = advance_flow(u, v, wet, count_wet(beside, level), half_turn)
+        new_u, new_v = advance_flow(
+            u, v, wet, count_wet(beside, level), half_turn, within
+        )
         moved = jnp.concatenate([turn(raw_t[:TILE], -1, 0), turn(raw_t[TILE:], 1, 0)], axis=0)
         lent = jnp.where(borrowed, moved, raw_u)
         strips_u = place(group, k, lent[:, cut[0]], lent[:, cut[1]], strips_u)
@@ -245,10 +264,6 @@
             item.wait()
         carried = lax.fori_loop(part.start, part.stop, body, carried, unroll=4)
     sum_u, sum_v, strips_u, strips_v = carried
-    starts = guess_ends[...]
-    others = blank
-    for number, value in enumerate((depth, starts)):
-        others = place(group, jnp.int32(number), value[:, cut[0]], value[:, cut[1]], others)
 
     def put(slot, low, high):
         a, b = swap(even, high, low)
@@ -260,29 +275,36 @@
         [is_sum_u(row[:TILE], False), is_sum_u(row[TILE:], True)], axis=0
     )
     moved = jnp.concatenate([turn(sum_v[:TILE], 4, 0), turn(sum_v[TILE:], 4, 0)], axis=0)
+    spare = starts[:TILE], starts[TILE:]
+    for shift, at, total in ((-2, TILE - 2, sum_u), (-1, TILE - 1, sum_v)):
+        spare = (
+            jnp.where(row[:TILE] == at, turn(total[:TILE], shift, 0), spare[0]),
+            jnp.where(
+                row[TILE:] == at - TILE + 2, turn(total[TILE:], shift + 3, 0), spare[1]
+            ),
+        )
+    starts = jnp.concatenate(spare, axis=0)
     whole = [depth, starts, jnp.where(first, sum_u, moved)]
     whole += [jnp.concatenate(pair, axis=1) for pair in (strips_u, strips_v, others)]
     for slot, value in enumerate(whole, KMT):
         put(slot, value[:TILE], value[TILE:])
     row = lax.broadcasted_iota(jnp.int32, (TILE, breadth), 0)
-    for field, first, width in ((0, U_ROWS, 2), (1, V_ROWS, 2), (2, T_ROWS, 1)):
-        each = TILE // width
-        for tile in range(levels // each):
+    for field, first in ((0, U_ROWS), (1, V_ROWS), (2, T_ROWS)):
+        for tile in range(levels // TILE):
             low = high = jnp.zeros((TILE, breadth), F32)
-            for q in range(each):
-                value = ends[field, tile * each + q]
-                here = row // width == q
-                low = jnp.where(here, turn(value[:TILE], width * q, 0), low)
-                high = jnp.where(here, turn(value[TILE:], width * (q + 1), 0), high)
+            for q in range(TILE):
+                value = ends[field, tile * TILE + q]
+                here = row == q
+                low = jnp.where(here, turn(value[:TILE], q, 0), low)
+                high = jnp.where(here, turn(value[TILE:], q + 1, 0), high)
             put(first + tile, low, high)
 
 
-def halo_rows(rows_even, rows_odd, first, width, k):
-    each = TILE // width
-    tile = first + k // each
+def halo_rows(rows_even, rows_odd, first, k):
+    tile = first + k // TILE
     north, south = swap(is_even("lat"), rows_even[tile], rows_odd[tile])
-    at = lax.rem(k, each) * width
-    south = pltpu.roll(south, lax.rem(2 * TILE - width - at, TILE), 0)
+    at = lax.rem(k, TILE)
+    south = pltpu.roll(south, lax.rem(2 * TILE - 1 - at, TILE), 0)
     north = pltpu.roll(north, lax.rem(TILE - at, TILE), 0)
     return south, north
 
@@ -311,14 +333,24 @@
         level = k.astype(F32)
         wet = depth > level
         count = count_wet(beside, level)
-        u_south, u_north = halo_rows(rows_even, rows_odd, U_ROWS, 2, k)
-        v_south, v_north = halo_rows(rows_even, rows_odd, V_ROWS, 2, k)
-        t_south, t_north = halo_rows(rows_even, rows_odd, T_ROWS, 1, k)
+        u_south, u_north = halo_rows(rows_even, rows_odd, U_ROWS, k)
+        v_south, v_north = halo_rows(rows_even, rows_odd, V_ROWS, k)
+        t_south, t_north = halo_rows(rows_even, rows_odd, T_ROWS, k)
         u = jnp.where(wet, stacked(u_south, state[0, k], u_north), 0.0)
         v = jnp.where(wet, stacked(v_south, state[1, k], v_north), 0.0)
         new_u, new_v = advance_flow(u, v, wet, count, half_turn)
-        flow_u[...] += new_u
-        flow_v[...] += new_v
+        flow_u[own] += new_u[own]
+        flow_v[own] += new_v[own]
+        for tile, inner, shift, sign in (
+            (slice(0, TILE), slice(TILE, 2 * TILE), -1, 1.0),
+            (slice(tall - TILE, tall), slice(tall - 2 * TILE, tall - TILE), 1, -1.0),
+        ):
+            open_to = turn(jnp.where(wet[inner], 1.0, 0.0), shift, 0)
+            across = sign * carry * v[tile]
+            for value, flow_sum in ((u, flow_u), (v, flow_v)):
+                other = turn(value[inner], shift, 0)
+                term = (time_step * viscosity) * (other - open_to * value[tile]) - across * other
+                flow_sum[tile] += jnp.where(wet[tile], term, 0.0)
         flow[0, k] = new_u[own]
         flow[1, k] = new_v[own]
         here = state[2, k]
@@ -339,11 +371,17 @@
     lax.fori_loop(0, levels, body, 0)
     row = lax.broadcasted_iota(jnp.int32, (tall, breadth), 0)
     outer = (row < TILE - 1) | (row > TILE + rows_here)
+    edge = (row == TILE - 1) | (row == TILE + rows_here)
     inner = jnp.zeros((rows_here, breadth), F32)
-    sums = halos(SUMS)
-    for shift, flow_sum in ((0, flow_u), (-4, flow_v)):
-        south, north = [turn(x, shift, 0) for x in sums]
-        flow_sum[...] = jnp.where(outer, stacked(south, inner, north), flow_sum[...])
+    sums, spare = halos(SUMS), halos(GUESS)
+    for number, flow_sum in enumerate((flow_u, flow_v)):
+        further = stacked(turn(sums[0], -4 * number, 0), inner, turn(sums[1], -4 * number, 0))
+        next_row = stacked(
+            turn(spare[0], -1 - number, 0), inner, turn(spare[1], 2 - number, 0)
+        )
+        total = flow_sum[...]
+        total = jnp.where(edge, total + next_row, total)
+        flow_sum[...] = jnp.where(outer, further, total)
 
 
 def fill_ends(x, west, east):
@@ -358,12 +396,6 @@
 
 def roll_to(x, source, target, k):
     return turn(x, target - source - TILE * k, 1)
-
-
-def over_groups(x):
-    for step in (TILE, 2 * TILE, 4 * TILE, 8 * TILE):
-        x = x + pltpu.roll(x, step, 1)
-    return x
 
 
 def krylov(
@@ -403,7 +435,7 @@
     )
     sums = []
     for side in range(2):
-        depth = over_groups(jnp.where(group == 0, other[side], 0.0))
+        depth = jnp.where(group == 1, turn(other[side], TILE, 1), other[side])
         wet = depth > level
         count = count_wet(around(depth), level)
         u = jnp.where(wet, u_sides[side], 0.0)
@@ -419,11 +451,23 @@
         edges[side, 0] = new_u[own]
         edges[side, 1] = new_v[own]
         edges[side, 2] = new_t[own]
-        sums.append((over_groups(new_u), over_groups(new_v), depth, turn(other[side], -TILE, 1)))
-
-    def assemble(field, number, seam):
-        west = turn(sums[0][number], -HALO, 1)
-        east = turn(sums[1][number], -2, 1)
+        sums.append((new_u, new_v))
+
+    def fold(x, step):
+        return x + turn(x, step, 1)
+
+    (u_west, v_west), (u_east, v_east) = [
+        [fold(x, LANES // 2) for x in side] for side in sums
+    ]
+    half = lane < LANES // 2
+    west = fold(jnp.where(half, u_west, v_west), LANES // 4)
+    east = fold(jnp.where(half, u_east, v_east), -LANES // 4)
+    quarter = lax.rem(lane // (LANES // 4), 2) == 1
+    folded = fold(fold(jnp.where(quarter, west, east), 2 * TILE), TILE)
+
+    def assemble(field, west, west_at, east, east_at, seam):
+        west = turn(west, -HALO - west_at, 1)
+        east = turn(east, -2 - east_at, 1)
         halo = jnp.where(lane < LANES // 2, east, west)
         tiles = [field[:, i : i + LANES] for i in range(0, breadth, LANES)]
         if seam:
@@ -435,10 +479,13 @@
         north, south = swap(lat_even, rows_even[slot], rows_odd[slot])
         return stacked(south, value, north)
 
-    wide_u = assemble(flow_u[...], 0, True)
-    wide_v = assemble(flow_v[...], 1, True)
-    wet_levels = assemble(tall_field(KMT, kmt[...].astype(F32)), 2, False)
-    first = assemble(tall_field(GUESS, guess[...]), 3, False)
+    last = LANES // 4 - TILE
+    wide_u = assemble(flow_u[...], folded, LANES // 4 + last, folded, last, True)
+    wide_v = assemble(flow_v[...], folded, 3 * LANES // 4 + last, folded, LANES // 2 + last, True)
+    wet_levels = assemble(
+        tall_field(KMT, kmt[...].astype(F32)), other[0], 0, other[1], 0, False
+    )
+    first = assemble(tall_field(GUESS, guess[...]), other[0], TILE, other[1], TILE, False)
 
     divergence = 0.5 * (east_of(wide_u) - west_of(wide_u)) + 0.5 * (
         north_of(wide_v) - south_of(wide_v)
@@ -520,10 +567,6 @@
             roll_to(edges[1, field], 1, LANES - 1, k),
         )
 
-    for c in range(chunks):
-        for k in range(c * size, (c + 1) * size):
-            done[2, k] = ended(tracer[k], 2, k)
-        send(2, 3, c).start()
     totals = jnp.sum(shares[...].reshape(-1, TILE, LANES), axis=0)
     for step in (1, 2, 4):
         totals = totals + turn(totals, step, 0)
@@ -552,6 +595,11 @@
             res_in = [r - step * (d - m) for r, d, m in zip(res_in, dir_in, moved)]
             dir_in = [r + ratio * d for r, d in zip(res_in, dir_in)]
 
+    for k in range(levels):
+        done[2, k] = ended(tracer[k], 2, k)
+    for c in range(chunks):
+        send(2, 3, c).start()
+
     def tile_of(i, j):
         cut = slice(i, i + TILE), slice(j, j + LANES)
         value = basis[0, *cut]

time: 48.9 us -> 48.1 us (0.984)
  waiting for transfers between devices: 1.56 us -> 0.41 us
    ppermute x2, waiting for transfers between devices: 1.56 us -> 0.41 us  [exchange(): return (lax.ppermute(to_even, axis, even), from_odd)]
where the time goes in v3:
time: 48.1 us; the launch traced here: 48 us
  blocking collectives  28.5 us (59%)
  Pallas kernels  9.33 us (19%)
  starting transfers between devices  8.95 us (19%)
  between operations  0.72 us (1%)
    all_to_all x1, blocking collectives, on_device(): shares = lax.all_to_all(shares, ('lon', 'lat'), 0, 0)  28.5 us
    ppermute x2, starting transfers between devices, exchange(): return (lax.ppermute(to_even, axis, even), from_odd)  6.66 us
    pallas_call x1, Pallas kernels, on_device(): pl.pallas_call(advance_inner, out_shape=[shape(2, levels, rows_here, brea...  2.66 us
    ppermute x2, starting transfers between devices, exchange(): from_odd = lax.ppermute(to_odd, axis, odd)  2.29 us
    pallas_call x1, Pallas kernels, on_device(): pl.pallas_call(pack_rows, in_specs=[hbm] * 3, out_specs=[vmem] * 2, out_s...  2.13 us
    pallas_call x1, Pallas kernels, on_device(): pl.pallas_call(pack_own, out_shape=shape(2, 4, rows_here, LANES), compile...  1.58 us
    pallas_call x1, Pallas kernels, on_device(): pl.pallas_call(krylov, out_shape=[shape(2, 3, rows_here, LANES), shape(IT...  1.48 us
    pallas_call x1, Pallas kernels, on_device(): pl.pallas_call(finish, in_specs=[vmem] * 6, out_specs=[hbm, hbm], out_sha...  1.46 us
  transfers between devices with their start and end apart: 4, of which 1 were waited for; matrix products, arithmetic and copies ran while one was open for 0% of the time, Pallas kernels for 9%

profile of v3, /device:TPU:1, one launch (start us, length us, event | category | flops | bytes accessed | tf_op | source)
XLA Modules:
  0.0 48.0 jit_solution(10135839461898959936)
XLA Ops:
  0.6 0.0 copy-start.1
  0.6 0.0 copy-start.2
  0.6 0.0 copy-start
  0.7 2.1 %shard_map.51 = (f32[12,8,256]{2,1,0:T(8,128)S(1)}, f32[12,8,256]{2,1,0:T(8,128)S(1)}) custom-call(f32[3,16,32,256]{3,2,1,0:T(8,128)} %state.5, s32[32,256]{1,0:T(8,128)} %kmt.9, f32[32,256]{1,0:T(8,128)} %guess.5), custom_call_target="tpu_custom_call" | custom-call | tf_op jit(solution)/shard_map/pallas_call | solution.py:661
  2.8 0.7 %collective-permute-start = (f32[12,8,256]{2,1,0:T(8,128)S(1)}, f32[12,8,256]{2,1,0:T(8,128)S(1)}, u32[]{:S(2)}, u32[]{:S(2)}) collective-permute-start(f32[12,8,256]{2,1,0:T(8,128)S(1)} %get-tuple-element.15), channel_id=1, source_target_pairs={{1,2},{2,1},{3,4},{4,3},{5,6},{6,5},{7,8},{8,7},{9,10},{10,9},{11,... | collective-permute-start | bytes 294920 | tf_op jit(solution)/shard_map/ppermute | solution.py:648
  3.5 4.8 %collective-permute-start.1 = (f32[12,8,256]{2,1,0:T(8,128)S(1)}, f32[12,8,256]{2,1,0:T(8,128)S(1)}, u32[]{:S(2)}, u32[]{:S(2)}) collective-permute-start(f32[12,8,256]{2,1,0:T(8,128)S(1)} %get-tuple-element.16), channel_id=1, source_target_pairs={{0,1},{1,0},{2,3},{3,2},{4,5},{5,4},{6,7},{7,6},{8,9},{9,8},{10,11... | collective-permute-start | bytes 294920 | tf_op jit(solution)/shard_map/ppermute | solution.py:649
  8.2 0.0 copy-done.1
  8.2 0.0 copy-done.2
  8.2 0.0 copy-done
  8.2 1.6 %shard_map.50.strips = f32[2,4,32,128]{3,2,1,0:T(8,128)S(1)} custom-call(f32[3,16,32,256]{3,2,1,0:T(8,128)S(1)} %copy-done, s32[32,256]{1,0:T(8,128)S(1)} %copy-done.1, f32[32,256]{1,0:T(8,128)S(1)} %copy-done.2), custom_call_target="tpu_custom_call" | custom-call | flops 23592960 | bytes 3145728 | tf_op jit(solution)/shard_map/pallas_call | solution.py:676
  9.8 0.0 collective-permute-done.rows_odd
  9.8 0.4 collective-permute-done.1.rows_even
  10.3 1.9 %collective-permute-start.3 = (f32[144,128]{1,0:T(8,128)S(1)}, f32[144,128]{1,0:T(8,128)S(1)}, u32[]{:S(2)}, u32[]{:S(2)}) collective-permute-start(f32[144,128]{1,0:T(8,128)S(1)} %get-tuple-element.17.sent_even), channel_id=1, source_target_pairs={{0,16},{16,0},{32,48},{48,32},{64,80},{80,64},{96,112},{112,96},{1... | collective-permute-start | bytes 221192 | tf_op jit(solution)/shard_map/ppermute | solution.py:649
  12.2 1.6 %collective-permute-start.2 = (f32[144,128]{1,0:T(8,128)S(1)}, f32[144,128]{1,0:T(8,128)S(1)}, u32[]{:S(2)}, u32[]{:S(2)}) collective-permute-start(f32[144,128]{1,0:T(8,128)S(1)} %get-tuple-element.18.sent_odd), channel_id=1, source_target_pairs={{16,32},{32,16},{48,64},{64,48},{80,96},{96,80},{112,128},{128,112... | collective-permute-start | bytes 221192 | tf_op jit(solution)/shard_map/ppermute | solution.py:648
  13.8 2.7 %shard_map.53 = (f32[2,16,32,256]{3,2,1,0:T(8,128)S(1)}, f32[16,32,256]{2,1,0:T(8,128)S(1)}, f32[48,256]{1,0:T(8,128)S(1)}, f32[48,256]{1,0:T(8,128)S(1)}, f32[48,128]{1,0:T(8,128)S(1)}) custom-call(f32[3,16,32,256]{3,2,1,0:T(8,128)S(1)} %copy-done, s32[32,256]{1,0:T(8,128)S(1)} %copy-done.1, f32[12,8,256]{2,1,0:T(8,128)S(1)} %collective-permute-done.rows_odd, ...), custom_call_target="tpu_custom_call" | custom-call | flops 23592960 | bytes 3145728 | tf_op jit(solution)/shard_map/pallas_call | solution.py:690
  16.5 0.0 collective-permute-done.3.got_even
  16.5 0.0 collective-permute-done.2.got_odd
  16.5 1.5 %shard_map.54 = (f32[2,3,32,128]{3,2,1,0:T(8,128)S(1)}, f32[5,48,384]{2,1,0:T(8,128)S(1)}, f32[1,128]{1,0:T(1,128)S(1)}) custom-call(f32[144,128]{1,0:T(8,128)S(1)} %get-tuple-element.17.sent_even, f32[144,128]{1,0:T(8,128)S(1)} %get-tuple-element.18.sent_odd, f32[144,128]{1,0:T(8,128)S(1)} %collective-permute-done.2.got_odd, ...), custom_call_target="tpu_custom_call" | custom-call | tf_op jit(solution)/shard_map/pallas_call | solution.py:703
  18.0 0.1 broadcast_in_dim.9
  18.0 28.5 %all_to_all.5 = f32[256,1,128]{2,1,0:T(1,128)S(1)} all-to-all(f32[256,1,128]{2,1,0:T(1,128)S(1)} %broadcast_in_dim.9), channel_id=1, replica_groups=mesh['lon'=16,'lat'=16] {'lon','lat'}, dimensions={0} | all-to-all | bytes 262144 | tf_op jit(solution)/shard_map/all_to_all | solution.py:717
  46.5 1.5 %shard_map.55 = (f32[3,16,32,256]{3,2,1,0:T(8,128)}, f32[32,256]{1,0:T(8,128)}) custom-call(f32[256,128]{1,0:T(8,128)S(1)} %bitcast.2, f32[5,48,384]{2,1,0:T(8,128)S(1)} %get-tuple-element.24.basis, f32[2,3,32,128]{3,2,1,0:T(8,128)S(1)} %get-tuple-element.25.edges, s32[32,256]{1,0:T(8,128)S(1)} %copy-done.1, f32[2,16,32,256]{3,2,1,0:T(8,128)S(1)} %get-tuple-element.26.flow, ...), custom_call_target="tpu_custom_call" | custom-call | tf_op jit(solution)/shard_map/pallas_call | solution.py:718
  (1 shorter events, 0.0 us)
Async XLA Ops:
  0.6 7.6 %copy-start.1 = (s32[32,256]{1,0:T(8,128)S(1)}, s32[32,256]{1,0:T(8,128)}, u32[]{:S(2)}) copy-start(s32[32,256]{1,0:T(8,128)} %kmt.9) | copy-start | bytes 98308
  0.6 7.6 %copy-start.2 = (f32[32,256]{1,0:T(8,128)S(1)}, f32[32,256]{1,0:T(8,128)}, u32[]{:S(2)}) copy-start(f32[32,256]{1,0:T(8,128)} %guess.5) | copy-start | bytes 98308
  0.6 7.6 %copy-start = (f32[3,16,32,256]{3,2,1,0:T(8,128)S(1)}, f32[3,16,32,256]{3,2,1,0:T(8,128)}, u32[]{:S(2)}) copy-start(f32[3,16,32,256]{3,2,1,0:T(8,128)} %state.5) | copy-start | bytes 4718596
  2.8 7.0 %collective-permute-start = (f32[12,8,256]{2,1,0:T(8,128)S(1)}, f32[12,8,256]{2,1,0:T(8,128)S(1)}, u32[]{:S(2)}, u32[]{:S(2)}) collective-permute-start(f32[12,8,256]{2,1,0:T(8,128)S(1)} %get-tuple-element.15), channel_id=1, source_target_pairs={{1,2},{2,1},{3,4},{4,3},{5,6},{6,5},{7,8},{8,7},{9,10},{10,9},{11,... | collective-permute-start | bytes 294920 | tf_op jit(solution)/shard_map/ppermute | solution.py:648
  3.5 6.8 %collective-permute-start.1 = (f32[12,8,256]{2,1,0:T(8,128)S(1)}, f32[12,8,256]{2,1,0:T(8,128)S(1)}, u32[]{:S(2)}, u32[]{:S(2)}) collective-permute-start(f32[12,8,256]{2,1,0:T(8,128)S(1)} %get-tuple-element.16), channel_id=1, source_target_pairs={{0,1},{1,0},{2,3},{3,2},{4,5},{5,4},{6,7},{7,6},{8,9},{9,8},{10,11... | collective-permute-start | bytes 294920 | tf_op jit(solution)/shard_map/ppermute | solution.py:649
  10.3 6.2 %collective-permute-start.3 = (f32[144,128]{1,0:T(8,128)S(1)}, f32[144,128]{1,0:T(8,128)S(1)}, u32[]{:S(2)}, u32[]{:S(2)}) collective-permute-start(f32[144,128]{1,0:T(8,128)S(1)} %get-tuple-element.17.sent_even), channel_id=1, source_target_pairs={{0,16},{16,0},{32,48},{48,32},{64,80},{80,64},{96,112},{112,96},{1... | collective-permute-start | bytes 221192 | tf_op jit(solution)/shard_map/ppermute | solution.py:649
  12.2 4.3 %collective-permute-start.2 = (f32[144,128]{1,0:T(8,128)S(1)}, f32[144,128]{1,0:T(8,128)S(1)}, u32[]{:S(2)}, u32[]{:S(2)}) collective-permute-start(f32[144,128]{1,0:T(8,128)S(1)} %get-tuple-element.18.sent_odd), channel_id=1, source_target_pairs={{16,32},{32,16},{48,64},{64,48},{80,96},{96,80},{112,128},{128,112... | collective-permute-start | bytes 221192 | tf_op jit(solution)/shard_map/ppermute | solution.py:648

commit v4 on v3

--- a/solution.py
+++ b/solution.py
@@ -547,6 +547,10 @@
     moments[...] = jnp.sum(total, axis=0, keepdims=True)
 
 
+def over(a, b):
+    return a / jnp.where(b > 1e-37, b, 1.0)
+
+
 def finish(shares, basis, edges, kmt, flow, tracer, out, pressure, done, held, sems, held_sem):
     levels, rows_here, breadth = tracer.shape
     own = slice(TILE, TILE + rows_here)
@@ -583,12 +587,12 @@
     dir_in = list(res_in)
     height_in = [zero] * ITERS
     for k in range(ITERS):
-        step = res[k] / (dirn[k] - dirn[k + 1])
+        step = over(res[k], dirn[k] - dirn[k + 1])
         step = jnp.clip(step, 1.0 / HIGHEST, 1.0 / LOWEST)
         height_in = [h + step * d for h, d in zip(height_in, dir_in)]
         if k + 1 < ITERS:
             new = [res[m] - step * (dirn[m] - dirn[m + 1]) for m in range(len(dirn) - 1)]
-            ratio = jnp.clip((step * (1.0 / res[k])) * new[k + 1], 0.0, HIGHEST / LOWEST)
+            ratio = jnp.clip(over(step, res[k]) * new[k + 1], 0.0, HIGHEST / LOWEST)
             dirn = [n + ratio * d for n, d in zip(new, dirn)]
             res = new
             moved = [zero] + dir_in[:-1]

time: 48.1 us -> 48.1 us (level)
  no operation moved by 1% of the time
where the time goes in v4:
time: 48.1 us; the launch traced here: 48 us
  blocking collectives  28.5 us (59%)
  Pallas kernels  9.32 us (19%)
  starting transfers between devices  8.95 us (19%)
  between operations  0.72 us (1%)
    all_to_all x1, blocking collectives, on_device(): shares = lax.all_to_all(shares, ('lon', 'lat'), 0, 0)  28.5 us
    ppermute x2, starting transfers between devices, exchange(): return (lax.ppermute(to_even, axis, even), from_odd)  6.66 us
    pallas_call x1, Pallas kernels, on_device(): pl.pallas_call(advance_inner, out_shape=[shape(2, levels, rows_here, brea...  2.66 us
    ppermute x2, starting transfers between devices, exchange(): from_odd = lax.ppermute(to_odd, axis, odd)  2.29 us
    pallas_call x1, Pallas kernels, on_device(): pl.pallas_call(pack_rows, in_specs=[hbm] * 3, out_specs=[vmem] * 2, out_s...  2.13 us
    pallas_call x1, Pallas kernels, on_device(): pl.pallas_call(pack_own, out_shape=shape(2, 4, rows_here, LANES), compile...  1.58 us
    pallas_call x1, Pallas kernels, on_device(): pl.pallas_call(krylov, out_shape=[shape(2, 3, rows_here, LANES), shape(IT...  1.48 us
    pallas_call x1, Pallas kernels, on_device(): pl.pallas_call(finish, in_specs=[vmem] * 6, out_specs=[hbm, hbm], out_sha...  1.46 us
  transfers between devices with their start and end apart: 4, of which 1 were waited for; matrix products, arithmetic and copies ran while one was open for 0% of the time, Pallas kernels for 9%

profile of v4, /device:TPU:1, one launch (start us, length us, event | category | flops | bytes accessed | tf_op | source)
XLA Modules:
  0.0 48.0 jit_solution(6130707735294291035)
XLA Ops:
  0.6 0.0 copy-start.1
  0.6 0.0 copy-start.2
  0.6 0.0 copy-start
  0.7 2.1 %shard_map.51 = (f32[12,8,256]{2,1,0:T(8,128)S(1)}, f32[12,8,256]{2,1,0:T(8,128)S(1)}) custom-call(f32[3,16,32,256]{3,2,1,0:T(8,128)} %state.5, s32[32,256]{1,0:T(8,128)} %kmt.9, f32[32,256]{1,0:T(8,128)} %guess.5), custom_call_target="tpu_custom_call" | custom-call | tf_op jit(solution)/shard_map/pallas_call | solution.py:665
  2.8 0.7 %collective-permute-start = (f32[12,8,256]{2,1,0:T(8,128)S(1)}, f32[12,8,256]{2,1,0:T(8,128)S(1)}, u32[]{:S(2)}, u32[]{:S(2)}) collective-permute-start(f32[12,8,256]{2,1,0:T(8,128)S(1)} %get-tuple-element.15), channel_id=1, source_target_pairs={{1,2},{2,1},{3,4},{4,3},{5,6},{6,5},{7,8},{8,7},{9,10},{10,9},{11,... | collective-permute-start | bytes 294920 | tf_op jit(solution)/shard_map/ppermute | solution.py:652
  3.5 4.8 %collective-permute-start.1 = (f32[12,8,256]{2,1,0:T(8,128)S(1)}, f32[12,8,256]{2,1,0:T(8,128)S(1)}, u32[]{:S(2)}, u32[]{:S(2)}) collective-permute-start(f32[12,8,256]{2,1,0:T(8,128)S(1)} %get-tuple-element.16), channel_id=1, source_target_pairs={{0,1},{1,0},{2,3},{3,2},{4,5},{5,4},{6,7},{7,6},{8,9},{9,8},{10,11... | collective-permute-start | bytes 294920 | tf_op jit(solution)/shard_map/ppermute | solution.py:653
  8.2 0.0 copy-done.1
  8.2 0.0 copy-done.2
  8.2 0.0 copy-done
  8.2 1.6 %shard_map.50.strips = f32[2,4,32,128]{3,2,1,0:T(8,128)S(1)} custom-call(f32[3,16,32,256]{3,2,1,0:T(8,128)S(1)} %copy-done, s32[32,256]{1,0:T(8,128)S(1)} %copy-done.1, f32[32,256]{1,0:T(8,128)S(1)} %copy-done.2), custom_call_target="tpu_custom_call" | custom-call | flops 23592960 | bytes 3145728 | tf_op jit(solution)/shard_map/pallas_call | solution.py:680
  9.8 0.0 collective-permute-done.rows_odd
  9.8 0.4 collective-permute-done.1.rows_even
  10.3 1.9 %collective-permute-start.3 = (f32[144,128]{1,0:T(8,128)S(1)}, f32[144,128]{1,0:T(8,128)S(1)}, u32[]{:S(2)}, u32[]{:S(2)}) collective-permute-start(f32[144,128]{1,0:T(8,128)S(1)} %get-tuple-element.17.sent_even), channel_id=1, source_target_pairs={{0,16},{16,0},{32,48},{48,32},{64,80},{80,64},{96,112},{112,96},{1... | collective-permute-start | bytes 221192 | tf_op jit(solution)/shard_map/ppermute | solution.py:653
  12.2 1.6 %collective-permute-start.2 = (f32[144,128]{1,0:T(8,128)S(1)}, f32[144,128]{1,0:T(8,128)S(1)}, u32[]{:S(2)}, u32[]{:S(2)}) collective-permute-start(f32[144,128]{1,0:T(8,128)S(1)} %get-tuple-element.18.sent_odd), channel_id=1, source_target_pairs={{16,32},{32,16},{48,64},{64,48},{80,96},{96,80},{112,128},{128,112... | collective-permute-start | bytes 221192 | tf_op jit(solution)/shard_map/ppermute | solution.py:652
  13.8 2.7 %shard_map.53 = (f32[2,16,32,256]{3,2,1,0:T(8,128)S(1)}, f32[16,32,256]{2,1,0:T(8,128)S(1)}, f32[48,256]{1,0:T(8,128)S(1)}, f32[48,256]{1,0:T(8,128)S(1)}, f32[48,128]{1,0:T(8,128)S(1)}) custom-call(f32[3,16,32,256]{3,2,1,0:T(8,128)S(1)} %copy-done, s32[32,256]{1,0:T(8,128)S(1)} %copy-done.1, f32[12,8,256]{2,1,0:T(8,128)S(1)} %collective-permute-done.rows_odd, ...), custom_call_target="tpu_custom_call" | custom-call | flops 23592960 | bytes 3145728 | tf_op jit(solution)/shard_map/pallas_call | solution.py:694
  16.5 0.0 collective-permute-done.3.got_even
  16.5 0.0 collective-permute-done.2.got_odd
  16.5 1.5 %shard_map.54 = (f32[2,3,32,128]{3,2,1,0:T(8,128)S(1)}, f32[5,48,384]{2,1,0:T(8,128)S(1)}, f32[1,128]{1,0:T(1,128)S(1)}) custom-call(f32[144,128]{1,0:T(8,128)S(1)} %get-tuple-element.17.sent_even, f32[144,128]{1,0:T(8,128)S(1)} %get-tuple-element.18.sent_odd, f32[144,128]{1,0:T(8,128)S(1)} %collective-permute-done.2.got_odd, ...), custom_call_target="tpu_custom_call" | custom-call | tf_op jit(solution)/shard_map/pallas_call | solution.py:707
  18.0 0.1 broadcast_in_dim.9
  18.0 28.5 %all_to_all.5 = f32[256,1,128]{2,1,0:T(1,128)S(1)} all-to-all(f32[256,1,128]{2,1,0:T(1,128)S(1)} %broadcast_in_dim.9), channel_id=1, replica_groups=mesh['lon'=16,'lat'=16] {'lon','lat'}, dimensions={0} | all-to-all | bytes 262144 | tf_op jit(solution)/shard_map/all_to_all | solution.py:721
  46.5 1.5 %shard_map.55 = (f32[3,16,32,256]{3,2,1,0:T(8,128)}, f32[32,256]{1,0:T(8,128)}) custom-call(f32[256,128]{1,0:T(8,128)S(1)} %bitcast.2, f32[5,48,384]{2,1,0:T(8,128)S(1)} %get-tuple-element.24.basis, f32[2,3,32,128]{3,2,1,0:T(8,128)S(1)} %get-tuple-element.25.edges, s32[32,256]{1,0:T(8,128)S(1)} %copy-done.1, f32[2,16,32,256]{3,2,1,0:T(8,128)S(1)} %get-tuple-element.26.flow, ...), custom_call_target="tpu_custom_call" | custom-call | tf_op jit(solution)/shard_map/pallas_call | solution.py:722
  (1 shorter events, 0.0 us)
Async XLA Ops:
  0.6 7.6 %copy-start.1 = (s32[32,256]{1,0:T(8,128)S(1)}, s32[32,256]{1,0:T(8,128)}, u32[]{:S(2)}) copy-start(s32[32,256]{1,0:T(8,128)} %kmt.9) | copy-start | bytes 98308
  0.6 7.6 %copy-start.2 = (f32[32,256]{1,0:T(8,128)S(1)}, f32[32,256]{1,0:T(8,128)}, u32[]{:S(2)}) copy-start(f32[32,256]{1,0:T(8,128)} %guess.5) | copy-start | bytes 98308
  0.6 7.6 %copy-start = (f32[3,16,32,256]{3,2,1,0:T(8,128)S(1)}, f32[3,16,32,256]{3,2,1,0:T(8,128)}, u32[]{:S(2)}) copy-start(f32[3,16,32,256]{3,2,1,0:T(8,128)} %state.5) | copy-start | bytes 4718596
  2.8 7.0 %collective-permute-start = (f32[12,8,256]{2,1,0:T(8,128)S(1)}, f32[12,8,256]{2,1,0:T(8,128)S(1)}, u32[]{:S(2)}, u32[]{:S(2)}) collective-permute-start(f32[12,8,256]{2,1,0:T(8,128)S(1)} %get-tuple-element.15), channel_id=1, source_target_pairs={{1,2},{2,1},{3,4},{4,3},{5,6},{6,5},{7,8},{8,7},{9,10},{10,9},{11,... | collective-permute-start | bytes 294920 | tf_op jit(solution)/shard_map/ppermute | solution.py:652
  3.5 6.8 %collective-permute-start.1 = (f32[12,8,256]{2,1,0:T(8,128)S(1)}, f32[12,8,256]{2,1,0:T(8,128)S(1)}, u32[]{:S(2)}, u32[]{:S(2)}) collective-permute-start(f32[12,8,256]{2,1,0:T(8,128)S(1)} %get-tuple-element.16), channel_id=1, source_target_pairs={{0,1},{1,0},{2,3},{3,2},{4,5},{5,4},{6,7},{7,6},{8,9},{9,8},{10,11... | collective-permute-start | bytes 294920 | tf_op jit(solution)/shard_map/ppermute | solution.py:653
  10.3 6.2 %collective-permute-start.3 = (f32[144,128]{1,0:T(8,128)S(1)}, f32[144,128]{1,0:T(8,128)S(1)}, u32[]{:S(2)}, u32[]{:S(2)}) collective-permute-start(f32[144,128]{1,0:T(8,128)S(1)} %get-tuple-element.17.sent_even), channel_id=1, source_target_pairs={{0,16},{16,0},{32,48},{48,32},{64,80},{80,64},{96,112},{112,96},{1... | collective-permute-start | bytes 221192 | tf_op jit(solution)/shard_map/ppermute | solution.py:653
  12.2 4.3 %collective-permute-start.2 = (f32[144,128]{1,0:T(8,128)S(1)}, f32[144,128]{1,0:T(8,128)S(1)}, u32[]{:S(2)}, u32[]{:S(2)}) collective-permute-start(f32[144,128]{1,0:T(8,128)S(1)} %get-tuple-element.18.sent_odd), channel_id=1, source_target_pairs={{16,32},{32,16},{48,64},{64,48},{80,96},{96,80},{112,128},{128,112... | collective-permute-start | bytes 221192 | tf_op jit(solution)/shard_map/ppermute | solution.py:652

commit v5 on v4

--- a/solution.py
+++ b/solution.py
@@ -34,6 +34,7 @@
 HIGHEST = 2.0 - LOWEST
 VMEM_LIMIT = 16 * 1024 * 1024
 VMEM_FIRST = 64520000
+VMEM_OWN = 60000000
 
 
 def params(limit=VMEM_LIMIT):
@@ -102,12 +103,19 @@
     return place(group, jnp.int32(1), guess[:, cut[0]], guess[:, cut[1]], wet)
 
 
-def pack_own(state, kmt, guess, strips):
+def pack_own(state_hbm, kmt, guess, state, strips, sems):
     levels, rows_here, breadth = state.shape[1:]
+    copies = [
+        pltpu.make_async_copy(state_hbm.at[field], state.at[field], sems.at[field])
+        for field in range(3)
+    ]
+    for item in copies:
+        item.start()
     group = lane_of((rows_here, LANES)) // TILE
     ends = slice(0, LANES), slice(breadth - LANES, breadth)
     blank = (jnp.zeros((rows_here, LANES), F32),) * 2
     for field in range(3):
+        copies[field].wait()
 
         def body(k, acc, field=field):
             west, east = [state[field, k, :, cols] for cols in ends]
@@ -571,7 +579,11 @@
             roll_to(edges[1, field], 1, LANES - 1, k),
         )
 
-    totals = jnp.sum(shares[...].reshape(-1, TILE, LANES), axis=0)
+    totals = shares[...]
+    while totals.shape[0] % (2 * TILE) == 0:
+        part = totals.shape[0] // 2
+        totals = totals[:part] + totals[part:]
+    totals = jnp.sum(totals.reshape(-1, TILE, LANES), axis=0)
     for step in (1, 2, 4):
         totals = totals + turn(totals, step, 0)
     lane = lane_of((TILE, LANES))
@@ -592,7 +604,7 @@
         height_in = [h + step * d for h, d in zip(height_in, dir_in)]
         if k + 1 < ITERS:
             new = [res[m] - step * (dirn[m] - dirn[m + 1]) for m in range(len(dirn) - 1)]
-            ratio = jnp.clip(over(step, res[k]) * new[k + 1], 0.0, HIGHEST / LOWEST)
+            ratio = jnp.clip((step * over(1.0, res[k])) * new[k + 1], 0.0, HIGHEST / LOWEST)
             dirn = [n + ratio * d for n, d in zip(new, dirn)]
             res = new
             moved = [zero] + dir_in[:-1]
@@ -677,10 +689,12 @@
     )(state, kmt, first_guess)
     rows_even, rows_odd = exchange("lat", to_even, to_odd)
 
-    strips = pl.pallas_call(
+    held, strips = pl.pallas_call(
         pack_own,
-        out_shape=shape(2, 4, rows_here, LANES),
-        compiler_params=params(),
+        in_specs=[hbm, vmem, vmem],
+        out_shape=[pltpu.VMEM(state.shape, F32), pltpu.VMEM((2, 4, rows_here, LANES), F32)],
+        scratch_shapes=[pltpu.SemaphoreType.DMA((3,))],
+        compiler_params=params(VMEM_OWN),
         cost_estimate=cost(state.size),
     )(state, kmt, first_guess)
     length = 3 * tall
@@ -702,7 +716,7 @@
         ],
         compiler_params=params(),
         cost_estimate=cost(state.size),
-    )(state, kmt, rows_odd, rows_even)
+    )(held, kmt, rows_odd, rows_even)
 
     edges, basis, moments = pl.pallas_call(
         krylov,

time: 48.1 us -> 48 us (level)
  blocking collectives: 28.5 us -> 24.4 us
  starting transfers between devices: 8.95 us -> 11.5 us
  Pallas kernels: 9.32 us -> 11.1 us
    all_to_all x1, blocking collectives: 28.5 us -> 24.4 us  [on_device(): shares = lax.all_to_all(shares, ('lon', 'lat'), 0, 0)]
    pallas_call x1, Pallas kernels: 1.58 us -> 3.43 us  [on_device(): pl.pallas_call(pack_own, in_specs=[hbm, vmem, vmem], out_shape=[pltpu.VME...]
    ppermute x2, starting transfers between devices: 6.66 us -> 7.96 us  [exchange(): return (lax.ppermute(to_even, axis, even), from_odd)]
    ppermute x2, starting transfers between devices: 2.29 us -> 3.51 us  [exchange(): from_odd = lax.ppermute(to_odd, axis, odd)]
  transfers between devices with their start and end apart: 4 -> 4, of which waited for: 1 -> 0; matrix products, arithmetic and copies ran while one was open for 0% -> 0% of each run, Pallas kernels for 9% -> 13%
where the time goes in v5:
time: 48 us; the launch traced here: 47.8 us
  blocking collectives  24.4 us (51%)
  starting transfers between devices  11.5 us (24%)
  Pallas kernels  11.1 us (23%)
  between operations  0.73 us (2%)
    all_to_all x1, blocking collectives, on_device(): shares = lax.all_to_all(shares, ('lon', 'lat'), 0, 0)  24.4 us
    ppermute x2, starting transfers between devices, exchange(): return (lax.ppermute(to_even, axis, even), from_odd)  7.96 us
    ppermute x2, starting transfers between devices, exchange(): from_odd = lax.ppermute(to_odd, axis, odd)  3.51 us
    pallas_call x1, Pallas kernels, on_device(): pl.pallas_call(pack_own, in_specs=[hbm, vmem, vmem], out_shape=[pltpu.VME...  3.43 us
    pallas_call x1, Pallas kernels, on_device(): pl.pallas_call(advance_inner, out_shape=[shape(2, levels, rows_here, brea...  2.68 us
    pallas_call x1, Pallas kernels, on_device(): pl.pallas_call(pack_rows, in_specs=[hbm] * 3, out_specs=[vmem] * 2, out_s...  2.03 us
    pallas_call x1, Pallas kernels, on_device(): pl.pallas_call(krylov, out_shape=[shape(2, 3, rows_here, LANES), shape(IT...  1.48 us
    pallas_call x1, Pallas kernels, on_device(): pl.pallas_call(finish, in_specs=[vmem] * 6, out_specs=[hbm, hbm], out_sha...  1.46 us
  transfers between devices with their start and end apart: 4, of which 0 were waited for; matrix products, arithmetic and copies ran while one was open for 0% of the time, Pallas kernels for 13%

profile of v5, /device:TPU:1, one launch (start us, length us, event | category | flops | bytes accessed | tf_op | source)
XLA Modules:
  0.0 47.8 jit_solution(14360239674012114531)
XLA Ops:
  0.6 0.0 copy-start
  0.6 2.0 %shard_map.51 = (f32[12,8,256]{2,1,0:T(8,128)S(1)}, f32[12,8,256]{2,1,0:T(8,128)S(1)}) custom-call(f32[3,16,32,256]{3,2,1,0:T(8,128)} %state.1, s32[32,256]{1,0:T(8,128)} %kmt.9, f32[32,256]{1,0:T(8,128)} %guess.5), custom_call_target="tpu_custom_call" | custom-call | tf_op jit(solution)/shard_map/pallas_call | solution.py:677
  2.7 0.7 %collective-permute-start = (f32[12,8,256]{2,1,0:T(8,128)S(1)}, f32[12,8,256]{2,1,0:T(8,128)S(1)}, u32[]{:S(2)}, u32[]{:S(2)}) collective-permute-start(f32[12,8,256]{2,1,0:T(8,128)S(1)} %get-tuple-element.18), channel_id=1, source_target_pairs={{1,2},{2,1},{3,4},{4,3},{5,6},{6,5},{7,8},{8,7},{9,10},{10,9},{11,... | collective-permute-start | bytes 294920 | tf_op jit(solution)/shard_map/ppermute | solution.py:664
  3.4 0.0 copy-start.1
  3.4 4.8 %collective-permute-start.1 = (f32[12,8,256]{2,1,0:T(8,128)S(1)}, f32[12,8,256]{2,1,0:T(8,128)S(1)}, u32[]{:S(2)}, u32[]{:S(2)}) collective-permute-start(f32[12,8,256]{2,1,0:T(8,128)S(1)} %get-tuple-element.19), channel_id=1, source_target_pairs={{0,1},{1,0},{2,3},{3,2},{4,5},{5,4},{6,7},{7,6},{8,9},{9,8},{10,11... | collective-permute-start | bytes 294920 | tf_op jit(solution)/shard_map/ppermute | solution.py:665
  8.1 3.4 %shard_map.50 = (f32[3,16,32,256]{3,2,1,0:T(8,128)S(1)}, f32[2,4,32,128]{3,2,1,0:T(8,128)S(1)}) custom-call(f32[3,16,32,256]{3,2,1,0:T(8,128)} %state.1, s32[32,256]{1,0:T(8,128)} %kmt.9, f32[32,256]{1,0:T(8,128)} %guess.5), custom_call_target="tpu_custom_call" | custom-call | flops 23592960 | bytes 3145728 | tf_op jit(solution)/shard_map/pallas_call | solution.py:692
  11.5 0.0 collective-permute-done.rows_odd
  11.6 0.0 collective-permute-done.1.rows_even
  11.6 2.8 %collective-permute-start.2 = (f32[144,128]{1,0:T(8,128)S(1)}, f32[144,128]{1,0:T(8,128)S(1)}, u32[]{:S(2)}, u32[]{:S(2)}) collective-permute-start(f32[144,128]{1,0:T(8,128)S(1)} %get-tuple-element.21.sent_odd), channel_id=1, source_target_pairs={{16,32},{32,16},{48,64},{64,48},{80,96},{96,80},{112,128},{128,112... | collective-permute-start | bytes 221192 | tf_op jit(solution)/shard_map/ppermute | solution.py:664
  14.5 3.2 %collective-permute-start.3 = (f32[144,128]{1,0:T(8,128)S(1)}, f32[144,128]{1,0:T(8,128)S(1)}, u32[]{:S(2)}, u32[]{:S(2)}) collective-permute-start(f32[144,128]{1,0:T(8,128)S(1)} %get-tuple-element.20.sent_even), channel_id=1, source_target_pairs={{0,16},{16,0},{32,48},{48,32},{64,80},{80,64},{96,112},{112,96},{1... | collective-permute-start | bytes 221192 | tf_op jit(solution)/shard_map/ppermute | solution.py:665
  17.7 0.0 copy-done
  17.7 2.7 %shard_map.53 = (f32[2,16,32,256]{3,2,1,0:T(8,128)S(1)}, f32[16,32,256]{2,1,0:T(8,128)S(1)}, f32[48,256]{1,0:T(8,128)S(1)}, f32[48,256]{1,0:T(8,128)S(1)}, f32[48,128]{1,0:T(8,128)S(1)}) custom-call(f32[3,16,32,256]{3,2,1,0:T(8,128)S(1)} %get-tuple-element.22.state, s32[32,256]{1,0:T(8,128)S(1)} %copy-done, f32[12,8,256]{2,1,0:T(8,128)S(1)} %collective-permute-done.rows_odd, ...), custom_call_target="tpu_custom_call" | custom-call | flops 23592960 | bytes 3145728 | tf_op jit(solution)/shard_map/pallas_call | solution.py:708
  20.4 0.0 collective-permute-done.2.got_odd
  20.4 0.0 collective-permute-done.3.got_even
  20.4 0.0 copy-done.1
  20.4 1.5 %shard_map.54 = (f32[2,3,32,128]{3,2,1,0:T(8,128)S(1)}, f32[5,48,384]{2,1,0:T(8,128)S(1)}, f32[1,128]{1,0:T(1,128)S(1)}) custom-call(f32[144,128]{1,0:T(8,128)S(1)} %get-tuple-element.20.sent_even, f32[144,128]{1,0:T(8,128)S(1)} %get-tuple-element.21.sent_odd, f32[144,128]{1,0:T(8,128)S(1)} %collective-permute-done.2.got_odd, ...), custom_call_target="tpu_custom_call" | custom-call | tf_op jit(solution)/shard_map/pallas_call | solution.py:721
  21.9 0.1 broadcast_in_dim.9
  22.0 24.4 %all_to_all.5 = f32[256,1,128]{2,1,0:T(1,128)S(1)} all-to-all(f32[256,1,128]{2,1,0:T(1,128)S(1)} %broadcast_in_dim.9), channel_id=1, replica_groups=mesh['lon'=16,'lat'=16] {'lon','lat'}, dimensions={0} | all-to-all | bytes 262144 | tf_op jit(solution)/shard_map/all_to_all | solution.py:735
  46.3 1.5 %shard_map.55 = (f32[3,16,32,256]{3,2,1,0:T(8,128)}, f32[32,256]{1,0:T(8,128)}) custom-call(f32[256,128]{1,0:T(8,128)S(1)} %bitcast.2, f32[5,48,384]{2,1,0:T(8,128)S(1)} %get-tuple-element.28.basis, f32[2,3,32,128]{3,2,1,0:T(8,128)S(1)} %get-tuple-element.29.edges, s32[32,256]{1,0:T(8,128)S(1)} %copy-done, f32[2,16,32,256]{3,2,1,0:T(8,128)S(1)} %get-tuple-element.30.flow, ...), custom_call_target="tpu_custom_call" | custom-call | tf_op jit(solution)/shard_map/pallas_call | solution.py:736
  (1 shorter events, 0.0 us)
Async XLA Ops:
  0.6 17.0 %copy-start = (s32[32,256]{1,0:T(8,128)S(1)}, s32[32,256]{1,0:T(8,128)}, u32[]{:S(2)}) copy-start(s32[32,256]{1,0:T(8,128)} %kmt.9) | copy-start | bytes 98308
  2.7 8.9 %collective-permute-start = (f32[12,8,256]{2,1,0:T(8,128)S(1)}, f32[12,8,256]{2,1,0:T(8,128)S(1)}, u32[]{:S(2)}, u32[]{:S(2)}) collective-permute-start(f32[12,8,256]{2,1,0:T(8,128)S(1)} %get-tuple-element.18), channel_id=1, source_target_pairs={{1,2},{2,1},{3,4},{4,3},{5,6},{6,5},{7,8},{8,7},{9,10},{10,9},{11,... | collective-permute-start | bytes 294920 | tf_op jit(solution)/shard_map/ppermute | solution.py:664
  3.4 17.0 %copy-start.1 = (f32[32,256]{1,0:T(8,128)S(1)}, f32[32,256]{1,0:T(8,128)}, u32[]{:S(2)}) copy-start(f32[32,256]{1,0:T(8,128)} %guess.5) | copy-start | bytes 98308
  3.4 8.2 %collective-permute-start.1 = (f32[12,8,256]{2,1,0:T(8,128)S(1)}, f32[12,8,256]{2,1,0:T(8,128)S(1)}, u32[]{:S(2)}, u32[]{:S(2)}) collective-permute-start(f32[12,8,256]{2,1,0:T(8,128)S(1)} %get-tuple-element.19), channel_id=1, source_target_pairs={{0,1},{1,0},{2,3},{3,2},{4,5},{5,4},{6,7},{7,6},{8,9},{9,8},{10,11... | collective-permute-start | bytes 294920 | tf_op jit(solution)/shard_map/ppermute | solution.py:665
  11.6 8.8 %collective-permute-start.2 = (f32[144,128]{1,0:T(8,128)S(1)}, f32[144,128]{1,0:T(8,128)S(1)}, u32[]{:S(2)}, u32[]{:S(2)}) collective-permute-start(f32[144,128]{1,0:T(8,128)S(1)} %get-tuple-element.21.sent_odd), channel_id=1, source_target_pairs={{16,32},{32,16},{48,64},{64,48},{80,96},{96,80},{112,128},{128,112... | collective-permute-start | bytes 221192 | tf_op jit(solution)/shard_map/ppermute | solution.py:664
  14.5 5.9 %collective-permute-start.3 = (f32[144,128]{1,0:T(8,128)S(1)}, f32[144,128]{1,0:T(8,128)S(1)}, u32[]{:S(2)}, u32[]{:S(2)}) collective-permute-start(f32[144,128]{1,0:T(8,128)S(1)} %get-tuple-element.20.sent_even), channel_id=1, source_target_pairs={{0,16},{16,0},{32,48},{48,32},{64,80},{80,64},{96,112},{112,96},{1... | collective-permute-start | bytes 221192 | tf_op jit(solution)/shard_map/ppermute | solution.py:665

commit v6 on v5

--- a/solution.py
+++ b/solution.py
@@ -114,6 +114,7 @@
     group = lane_of((rows_here, LANES)) // TILE
     ends = slice(0, LANES), slice(breadth - LANES, breadth)
     blank = (jnp.zeros((rows_here, LANES), F32),) * 2
+    strips[0, 3], strips[1, 3] = pack_others(group, kmt[...].astype(F32), guess[...], ends)
     for field in range(3):
         copies[field].wait()
 
@@ -126,7 +127,6 @@
     slot = lax.rem(lane_of((rows_here, LANES)), TILE)
     strips[0, 0] = jnp.where(slot == 1, turn(strips[0, 2], -1, 1), strips[0, 0])
     strips[1, 0] = jnp.where(slot == HALO, turn(strips[1, 2], 1, 1), strips[1, 0])
-    strips[0, 3], strips[1, 3] = pack_others(group, kmt[...].astype(F32), guess[...], ends)
 
 
 def pack_cols(strips, rows_odd, rows_even, msg_odd, msg_even, own_tracer):

time: 48 us -> 48 us (level)
  transfers between devices with their start and end apart: 4 -> 4, of which waited for: 0 -> 0; matrix products, arithmetic and copies ran while one was open for 0% -> 0% of each run, Pallas kernels for 13% -> 12%
where the time goes in v6:
time: 48 us; the launch traced here: 47.8 us
  blocking collectives  24.7 us (51%)
  starting transfers between devices  11.5 us (24%)
  Pallas kernels  10.8 us (22%)
  between operations  0.73 us (2%)
    all_to_all x1, blocking collectives, on_device(): shares = lax.all_to_all(shares, ('lon', 'lat'), 0, 0)  24.7 us
    ppermute x2, starting transfers between devices, exchange(): return (lax.ppermute(to_even, axis, even), from_odd)  7.96 us
    ppermute x2, starting transfers between devices, exchange(): from_odd = lax.ppermute(to_odd, axis, odd)  3.51 us
    pallas_call x1, Pallas kernels, on_device(): pl.pallas_call(pack_own, in_specs=[hbm, vmem, vmem], out_shape=[pltpu.VME...  3.14 us
    pallas_call x1, Pallas kernels, on_device(): pl.pallas_call(advance_inner, out_shape=[shape(2, levels, rows_here, brea...  2.68 us
    pallas_call x1, Pallas kernels, on_device(): pl.pallas_call(pack_rows, in_specs=[hbm] * 3, out_specs=[vmem] * 2, out_s...  2.03 us
    pallas_call x1, Pallas kernels, on_device(): pl.pallas_call(krylov, out_shape=[shape(2, 3, rows_here, LANES), shape(IT...  1.48 us
    pallas_call x1, Pallas kernels, on_device(): pl.pallas_call(finish, in_specs=[vmem] * 6, out_specs=[hbm, hbm], out_sha...  1.46 us
  transfers between devices with their start and end apart: 4, of which 0 were waited for; matrix products, arithmetic and copies ran while one was open for 0% of the time, Pallas kernels for 12%

profile of v6, /device:TPU:1, one launch (start us, length us, event | category | flops | bytes accessed | tf_op | source)
XLA Modules:
  0.0 47.8 jit_solution(16820429657878778471)
XLA Ops:
  0.6 0.0 copy-start
  0.6 2.0 %shard_map.51 = (f32[12,8,256]{2,1,0:T(8,128)S(1)}, f32[12,8,256]{2,1,0:T(8,128)S(1)}) custom-call(f32[3,16,32,256]{3,2,1,0:T(8,128)} %state.1, s32[32,256]{1,0:T(8,128)} %kmt.9, f32[32,256]{1,0:T(8,128)} %guess.5), custom_call_target="tpu_custom_call" | custom-call | tf_op jit(solution)/shard_map/pallas_call | solution.py:677
  2.7 0.7 %collective-permute-start = (f32[12,8,256]{2,1,0:T(8,128)S(1)}, f32[12,8,256]{2,1,0:T(8,128)S(1)}, u32[]{:S(2)}, u32[]{:S(2)}) collective-permute-start(f32[12,8,256]{2,1,0:T(8,128)S(1)} %get-tuple-element.18), channel_id=1, source_target_pairs={{1,2},{2,1},{3,4},{4,3},{5,6},{6,5},{7,8},{8,7},{9,10},{10,9},{11,... | collective-permute-start | bytes 294920 | tf_op jit(solution)/shard_map/ppermute | solution.py:664
  3.4 0.0 copy-start.1
  3.4 4.8 %collective-permute-start.1 = (f32[12,8,256]{2,1,0:T(8,128)S(1)}, f32[12,8,256]{2,1,0:T(8,128)S(1)}, u32[]{:S(2)}, u32[]{:S(2)}) collective-permute-start(f32[12,8,256]{2,1,0:T(8,128)S(1)} %get-tuple-element.19), channel_id=1, source_target_pairs={{0,1},{1,0},{2,3},{3,2},{4,5},{5,4},{6,7},{7,6},{8,9},{9,8},{10,11... | collective-permute-start | bytes 294920 | tf_op jit(solution)/shard_map/ppermute | solution.py:665
  8.1 3.1 %shard_map.50 = (f32[3,16,32,256]{3,2,1,0:T(8,128)S(1)}, f32[2,4,32,128]{3,2,1,0:T(8,128)S(1)}) custom-call(f32[3,16,32,256]{3,2,1,0:T(8,128)} %state.1, s32[32,256]{1,0:T(8,128)} %kmt.9, f32[32,256]{1,0:T(8,128)} %guess.5), custom_call_target="tpu_custom_call" | custom-call | flops 23592960 | bytes 3145728 | tf_op jit(solution)/shard_map/pallas_call | solution.py:692
  11.3 0.0 collective-permute-done.rows_odd
  11.3 0.0 collective-permute-done.1.rows_even
  11.3 2.8 %collective-permute-start.2 = (f32[144,128]{1,0:T(8,128)S(1)}, f32[144,128]{1,0:T(8,128)S(1)}, u32[]{:S(2)}, u32[]{:S(2)}) collective-permute-start(f32[144,128]{1,0:T(8,128)S(1)} %get-tuple-element.21.sent_odd), channel_id=1, source_target_pairs={{16,32},{32,16},{48,64},{64,48},{80,96},{96,80},{112,128},{128,112... | collective-permute-start | bytes 221192 | tf_op jit(solution)/shard_map/ppermute | solution.py:664
  14.2 3.2 %collective-permute-start.3 = (f32[144,128]{1,0:T(8,128)S(1)}, f32[144,128]{1,0:T(8,128)S(1)}, u32[]{:S(2)}, u32[]{:S(2)}) collective-permute-start(f32[144,128]{1,0:T(8,128)S(1)} %get-tuple-element.20.sent_even), channel_id=1, source_target_pairs={{0,16},{16,0},{32,48},{48,32},{64,80},{80,64},{96,112},{112,96},{1... | collective-permute-start | bytes 221192 | tf_op jit(solution)/shard_map/ppermute | solution.py:665
  17.4 0.0 copy-done
  17.4 2.7 %shard_map.53 = (f32[2,16,32,256]{3,2,1,0:T(8,128)S(1)}, f32[16,32,256]{2,1,0:T(8,128)S(1)}, f32[48,256]{1,0:T(8,128)S(1)}, f32[48,256]{1,0:T(8,128)S(1)}, f32[48,128]{1,0:T(8,128)S(1)}) custom-call(f32[3,16,32,256]{3,2,1,0:T(8,128)S(1)} %get-tuple-element.22.state, s32[32,256]{1,0:T(8,128)S(1)} %copy-done, f32[12,8,256]{2,1,0:T(8,128)S(1)} %collective-permute-done.rows_odd, ...), custom_call_target="tpu_custom_call" | custom-call | flops 23592960 | bytes 3145728 | tf_op jit(solution)/shard_map/pallas_call | solution.py:708
  20.1 0.0 collective-permute-done.2.got_odd
  20.1 0.0 collective-permute-done.3.got_even
  20.1 0.0 copy-done.1
  20.1 1.5 %shard_map.54 = (f32[2,3,32,128]{3,2,1,0:T(8,128)S(1)}, f32[5,48,384]{2,1,0:T(8,128)S(1)}, f32[1,128]{1,0:T(1,128)S(1)}) custom-call(f32[144,128]{1,0:T(8,128)S(1)} %get-tuple-element.20.sent_even, f32[144,128]{1,0:T(8,128)S(1)} %get-tuple-element.21.sent_odd, f32[144,128]{1,0:T(8,128)S(1)} %collective-permute-done.2.got_odd, ...), custom_call_target="tpu_custom_call" | custom-call | tf_op jit(solution)/shard_map/pallas_call | solution.py:721
  21.6 0.1 broadcast_in_dim.9
  21.7 24.7 %all_to_all.5 = f32[256,1,128]{2,1,0:T(1,128)S(1)} all-to-all(f32[256,1,128]{2,1,0:T(1,128)S(1)} %broadcast_in_dim.9), channel_id=1, replica_groups=mesh['lon'=16,'lat'=16] {'lon','lat'}, dimensions={0} | all-to-all | bytes 262144 | tf_op jit(solution)/shard_map/all_to_all | solution.py:735
  46.3 1.5 %shard_map.55 = (f32[3,16,32,256]{3,2,1,0:T(8,128)}, f32[32,256]{1,0:T(8,128)}) custom-call(f32[256,128]{1,0:T(8,128)S(1)} %bitcast.2, f32[5,48,384]{2,1,0:T(8,128)S(1)} %get-tuple-element.28.basis, f32[2,3,32,128]{3,2,1,0:T(8,128)S(1)} %get-tuple-element.29.edges, s32[32,256]{1,0:T(8,128)S(1)} %copy-done, f32[2,16,32,256]{3,2,1,0:T(8,128)S(1)} %get-tuple-element.30.flow, ...), custom_call_target="tpu_custom_call" | custom-call | tf_op jit(solution)/shard_map/pallas_call | solution.py:736
  (1 shorter events, 0.0 us)
Async XLA Ops:
  0.6 16.8 %copy-start = (s32[32,256]{1,0:T(8,128)S(1)}, s32[32,256]{1,0:T(8,128)}, u32[]{:S(2)}) copy-start(s32[32,256]{1,0:T(8,128)} %kmt.9) | copy-start | bytes 98308
  2.7 8.6 %collective-permute-start = (f32[12,8,256]{2,1,0:T(8,128)S(1)}, f32[12,8,256]{2,1,0:T(8,128)S(1)}, u32[]{:S(2)}, u32[]{:S(2)}) collective-permute-start(f32[12,8,256]{2,1,0:T(8,128)S(1)} %get-tuple-element.18), channel_id=1, source_target_pairs={{1,2},{2,1},{3,4},{4,3},{5,6},{6,5},{7,8},{8,7},{9,10},{10,9},{11,... | collective-permute-start | bytes 294920 | tf_op jit(solution)/shard_map/ppermute | solution.py:664
  3.4 16.7 %copy-start.1 = (f32[32,256]{1,0:T(8,128)S(1)}, f32[32,256]{1,0:T(8,128)}, u32[]{:S(2)}) copy-start(f32[32,256]{1,0:T(8,128)} %guess.5) | copy-start | bytes 98308
  3.4 7.9 %collective-permute-start.1 = (f32[12,8,256]{2,1,0:T(8,128)S(1)}, f32[12,8,256]{2,1,0:T(8,128)S(1)}, u32[]{:S(2)}, u32[]{:S(2)}) collective-permute-start(f32[12,8,256]{2,1,0:T(8,128)S(1)} %get-tuple-element.19), channel_id=1, source_target_pairs={{0,1},{1,0},{2,3},{3,2},{4,5},{5,4},{6,7},{7,6},{8,9},{9,8},{10,11... | collective-permute-start | bytes 294920 | tf_op jit(solution)/shard_map/ppermute | solution.py:665
  11.3 8.8 %collective-permute-start.2 = (f32[144,128]{1,0:T(8,128)S(1)}, f32[144,128]{1,0:T(8,128)S(1)}, u32[]{:S(2)}, u32[]{:S(2)}) collective-permute-start(f32[144,128]{1,0:T(8,128)S(1)} %get-tuple-element.21.sent_odd), channel_id=1, source_target_pairs={{16,32},{32,16},{48,64},{64,48},{80,96},{96,80},{112,128},{128,112... | collective-permute-start | bytes 221192 | tf_op jit(solution)/shard_map/ppermute | solution.py:664
  14.2 5.9 %collective-permute-start.3 = (f32[144,128]{1,0:T(8,128)S(1)}, f32[144,128]{1,0:T(8,128)S(1)}, u32[]{:S(2)}, u32[]{:S(2)}) collective-permute-start(f32[144,128]{1,0:T(8,128)S(1)} %get-tuple-element.20.sent_even), channel_id=1, source_target_pairs={{0,16},{16,0},{32,48},{48,32},{64,80},{80,64},{96,112},{112,96},{1... | collective-permute-start | bytes 221192 | tf_op jit(solution)/shard_map/ppermute | solution.py:665

commit v7 on v5

--- a/solution.py
+++ b/solution.py
@@ -376,7 +376,7 @@
         )
         return 0
 
-    lax.fori_loop(0, levels, body, 0)
+    lax.fori_loop(0, levels, body, 0, unroll=2)
     row = lax.broadcasted_iota(jnp.int32, (tall, breadth), 0)
     outer = (row < TILE - 1) | (row > TILE + rows_here)
     edge = (row == TILE - 1) | (row == TILE + rows_here)

time: 48 us -> 48 us (level)
  transfers between devices with their start and end apart: 4 -> 4, of which waited for: 0 -> 0; matrix products, arithmetic and copies ran while one was open for 0% -> 0% of each run, Pallas kernels for 13% -> 12%
where the time goes in v7:
time: 48 us; the launch traced here: 47.8 us
  blocking collectives  24.7 us (51%)
  starting transfers between devices  11.5 us (24%)
  Pallas kernels  10.8 us (22%)
  between operations  0.73 us (2%)
    all_to_all x1, blocking collectives, on_device(): shares = lax.all_to_all(shares, ('lon', 'lat'), 0, 0)  24.7 us
    ppermute x2, starting transfers between devices, exchange(): return (lax.ppermute(to_even, axis, even), from_odd)  7.96 us
    ppermute x2, starting transfers between devices, exchange(): from_odd = lax.ppermute(to_odd, axis, odd)  3.51 us
    pallas_call x1, Pallas kernels, on_device(): pl.pallas_call(pack_own, in_specs=[hbm, vmem, vmem], out_shape=[pltpu.VME...  3.43 us
    pallas_call x1, Pallas kernels, on_device(): pl.pallas_call(advance_inner, out_shape=[shape(2, levels, rows_here, brea...  2.38 us
    pallas_call x1, Pallas kernels, on_device(): pl.pallas_call(pack_rows, in_specs=[hbm] * 3, out_specs=[vmem] * 2, out_s...  2.03 us
    pallas_call x1, Pallas kernels, on_device(): pl.pallas_call(krylov, out_shape=[shape(2, 3, rows_here, LANES), shape(IT...  1.48 us
    pallas_call x1, Pallas kernels, on_device(): pl.pallas_call(finish, in_specs=[vmem] * 6, out_specs=[hbm, hbm], out_sha...  1.46 us
  transfers between devices with their start and end apart: 4, of which 0 were waited for; matrix products, arithmetic and copies ran while one was open for 0% of the time, Pallas kernels for 12%

profile of v7, /device:TPU:1, one launch (start us, length us, event | category | flops | bytes accessed | tf_op | source)
XLA Modules:
  0.0 47.8 jit_solution(11645148166779401883)
XLA Ops:
  0.6 0.0 copy-start
  0.6 2.0 %shard_map.51 = (f32[12,8,256]{2,1,0:T(8,128)S(1)}, f32[12,8,256]{2,1,0:T(8,128)S(1)}) custom-call(f32[3,16,32,256]{3,2,1,0:T(8,128)} %state.1, s32[32,256]{1,0:T(8,128)} %kmt.9, f32[32,256]{1,0:T(8,128)} %guess.5), custom_call_target="tpu_custom_call" | custom-call | tf_op jit(solution)/shard_map/pallas_call | solution.py:677
  2.7 0.7 %collective-permute-start = (f32[12,8,256]{2,1,0:T(8,128)S(1)}, f32[12,8,256]{2,1,0:T(8,128)S(1)}, u32[]{:S(2)}, u32[]{:S(2)}) collective-permute-start(f32[12,8,256]{2,1,0:T(8,128)S(1)} %get-tuple-element.18), channel_id=1, source_target_pairs={{1,2},{2,1},{3,4},{4,3},{5,6},{6,5},{7,8},{8,7},{9,10},{10,9},{11,... | collective-permute-start | bytes 294920 | tf_op jit(solution)/shard_map/ppermute | solution.py:664
  3.4 0.0 copy-start.1
  3.4 4.8 %collective-permute-start.1 = (f32[12,8,256]{2,1,0:T(8,128)S(1)}, f32[12,8,256]{2,1,0:T(8,128)S(1)}, u32[]{:S(2)}, u32[]{:S(2)}) collective-permute-start(f32[12,8,256]{2,1,0:T(8,128)S(1)} %get-tuple-element.19), channel_id=1, source_target_pairs={{0,1},{1,0},{2,3},{3,2},{4,5},{5,4},{6,7},{7,6},{8,9},{9,8},{10,11... | collective-permute-start | bytes 294920 | tf_op jit(solution)/shard_map/ppermute | solution.py:665
  8.1 3.4 %shard_map.50 = (f32[3,16,32,256]{3,2,1,0:T(8,128)S(1)}, f32[2,4,32,128]{3,2,1,0:T(8,128)S(1)}) custom-call(f32[3,16,32,256]{3,2,1,0:T(8,128)} %state.1, s32[32,256]{1,0:T(8,128)} %kmt.9, f32[32,256]{1,0:T(8,128)} %guess.5), custom_call_target="tpu_custom_call" | custom-call | flops 23592960 | bytes 3145728 | tf_op jit(solution)/shard_map/pallas_call | solution.py:692
  11.5 0.0 collective-permute-done.rows_odd
  11.6 0.0 collective-permute-done.1.rows_even
  11.6 2.8 %collective-permute-start.2 = (f32[144,128]{1,0:T(8,128)S(1)}, f32[144,128]{1,0:T(8,128)S(1)}, u32[]{:S(2)}, u32[]{:S(2)}) collective-permute-start(f32[144,128]{1,0:T(8,128)S(1)} %get-tuple-element.21.sent_odd), channel_id=1, source_target_pairs={{16,32},{32,16},{48,64},{64,48},{80,96},{96,80},{112,128},{128,112... | collective-permute-start | bytes 221192 | tf_op jit(solution)/shard_map/ppermute | solution.py:664
  14.5 3.2 %collective-permute-start.3 = (f32[144,128]{1,0:T(8,128)S(1)}, f32[144,128]{1,0:T(8,128)S(1)}, u32[]{:S(2)}, u32[]{:S(2)}) collective-permute-start(f32[144,128]{1,0:T(8,128)S(1)} %get-tuple-element.20.sent_even), channel_id=1, source_target_pairs={{0,16},{16,0},{32,48},{48,32},{64,80},{80,64},{96,112},{112,96},{1... | collective-permute-start | bytes 221192 | tf_op jit(solution)/shard_map/ppermute | solution.py:665
  17.7 0.0 copy-done
  17.7 2.4 %shard_map.53 = (f32[2,16,32,256]{3,2,1,0:T(8,128)S(1)}, f32[16,32,256]{2,1,0:T(8,128)S(1)}, f32[48,256]{1,0:T(8,128)S(1)}, f32[48,256]{1,0:T(8,128)S(1)}, f32[48,128]{1,0:T(8,128)S(1)}) custom-call(f32[3,16,32,256]{3,2,1,0:T(8,128)S(1)} %get-tuple-element.22.state, s32[32,256]{1,0:T(8,128)S(1)} %copy-done, f32[12,8,256]{2,1,0:T(8,128)S(1)} %collective-permute-done.rows_odd, ...), custom_call_target="tpu_custom_call" | custom-call | flops 23592960 | bytes 3145728 | tf_op jit(solution)/shard_map/pallas_call | solution.py:708
  20.0 0.0 collective-permute-done.2.got_odd
  20.1 0.0 collective-permute-done.3.got_even
  20.1 0.0 copy-done.1
  20.1 1.5 %shard_map.54 = (f32[2,3,32,128]{3,2,1,0:T(8,128)S(1)}, f32[5,48,384]{2,1,0:T(8,128)S(1)}, f32[1,128]{1,0:T(1,128)S(1)}) custom-call(f32[144,128]{1,0:T(8,128)S(1)} %get-tuple-element.20.sent_even, f32[144,128]{1,0:T(8,128)S(1)} %get-tuple-element.21.sent_odd, f32[144,128]{1,0:T(8,128)S(1)} %collective-permute-done.2.got_odd, ...), custom_call_target="tpu_custom_call" | custom-call | tf_op jit(solution)/shard_map/pallas_call | solution.py:721
  21.6 0.1 broadcast_in_dim.9
  21.6 24.7 %all_to_all.5 = f32[256,1,128]{2,1,0:T(1,128)S(1)} all-to-all(f32[256,1,128]{2,1,0:T(1,128)S(1)} %broadcast_in_dim.9), channel_id=1, replica_groups=mesh['lon'=16,'lat'=16] {'lon','lat'}, dimensions={0} | all-to-all | bytes 262144 | tf_op jit(solution)/shard_map/all_to_all | solution.py:735
  46.3 1.5 %shard_map.55 = (f32[3,16,32,256]{3,2,1,0:T(8,128)}, f32[32,256]{1,0:T(8,128)}) custom-call(f32[256,128]{1,0:T(8,128)S(1)} %bitcast.2, f32[5,48,384]{2,1,0:T(8,128)S(1)} %get-tuple-element.28.basis, f32[2,3,32,128]{3,2,1,0:T(8,128)S(1)} %get-tuple-element.29.edges, s32[32,256]{1,0:T(8,128)S(1)} %copy-done, f32[2,16,32,256]{3,2,1,0:T(8,128)S(1)} %get-tuple-element.30.flow, ...), custom_call_target="tpu_custom_call" | custom-call | tf_op jit(solution)/shard_map/pallas_call | solution.py:736
  (1 shorter events, 0.0 us)
Async XLA Ops:
  0.6 17.0 %copy-start = (s32[32,256]{1,0:T(8,128)S(1)}, s32[32,256]{1,0:T(8,128)}, u32[]{:S(2)}) copy-start(s32[32,256]{1,0:T(8,128)} %kmt.9) | copy-start | bytes 98308
  2.7 8.9 %collective-permute-start = (f32[12,8,256]{2,1,0:T(8,128)S(1)}, f32[12,8,256]{2,1,0:T(8,128)S(1)}, u32[]{:S(2)}, u32[]{:S(2)}) collective-permute-start(f32[12,8,256]{2,1,0:T(8,128)S(1)} %get-tuple-element.18), channel_id=1, source_target_pairs={{1,2},{2,1},{3,4},{4,3},{5,6},{6,5},{7,8},{8,7},{9,10},{10,9},{11,... | collective-permute-start | bytes 294920 | tf_op jit(solution)/shard_map/ppermute | solution.py:664
  3.4 16.7 %copy-start.1 = (f32[32,256]{1,0:T(8,128)S(1)}, f32[32,256]{1,0:T(8,128)}, u32[]{:S(2)}) copy-start(f32[32,256]{1,0:T(8,128)} %guess.5) | copy-start | bytes 98308
  3.4 8.2 %collective-permute-start.1 = (f32[12,8,256]{2,1,0:T(8,128)S(1)}, f32[12,8,256]{2,1,0:T(8,128)S(1)}, u32[]{:S(2)}, u32[]{:S(2)}) collective-permute-start(f32[12,8,256]{2,1,0:T(8,128)S(1)} %get-tuple-element.19), channel_id=1, source_target_pairs={{0,1},{1,0},{2,3},{3,2},{4,5},{5,4},{6,7},{7,6},{8,9},{9,8},{10,11... | collective-permute-start | bytes 294920 | tf_op jit(solution)/shard_map/ppermute | solution.py:665
  11.6 8.4 %collective-permute-start.2 = (f32[144,128]{1,0:T(8,128)S(1)}, f32[144,128]{1,0:T(8,128)S(1)}, u32[]{:S(2)}, u32[]{:S(2)}) collective-permute-start(f32[144,128]{1,0:T(8,128)S(1)} %get-tuple-element.21.sent_odd), channel_id=1, source_target_pairs={{16,32},{32,16},{48,64},{64,48},{80,96},{96,80},{112,128},{128,112... | collective-permute-start | bytes 221192 | tf_op jit(solution)/shard_map/ppermute | solution.py:664
  14.5 5.6 %collective-permute-start.3 = (f32[144,128]{1,0:T(8,128)S(1)}, f32[144,128]{1,0:T(8,128)S(1)}, u32[]{:S(2)}, u32[]{:S(2)}) collective-permute-start(f32[144,128]{1,0:T(8,128)S(1)} %get-tuple-element.20.sent_even), channel_id=1, source_target_pairs={{0,16},{16,0},{32,48},{48,32},{64,80},{80,64},{96,112},{112,96},{1... | collective-permute-start | bytes 221192 | tf_op jit(solution)/shard_map/ppermute | solution.py:665
